TPU v7x, 128 devices: a whole 4x4x4 slice. The times are simulated.
128 devices in a mesh: len: 8 (over y, core), hgt: 16 (over x, z).
Axes of the slice: x: 4, y: 4, z: 4, core: 2. Of those that a mesh axis runs over, the one named last changes fastest.
Arguments:
- air_temp: float32 [64, 128, 256], P('len', 'hgt'), may hold values from -6 to 6
- velocity: float32 [64, 128, 256], P('len', 'hgt'), may hold values from -1 to 1
- fluid: int32 [64, 128, 256], P('len', 'hgt'), may hold values 0 or 1
- enthalpy: float32 [4096, 128], P(('len', 'hgt')), may hold values from -1 to 3
- adjacency_lists: int32 [4096, 8, 128], P(('len', 'hgt')), may hold values from 0 to 127
- send_cells: int32 [128, 128, 256], P(('len', 'hgt')), may hold values from 0 to 16383
- contact: float32 [128, 128, 256], P(('len', 'hgt')), may hold values from 0.2 to 2
- pair_rows: int32 [128, 128], P(('len', 'hgt')), may hold values from 0 to 256, as said below
- recv_nodes: int32 [128, 128, 256], P(('len', 'hgt')), may hold values from 0 to 4095
Outputs:
- air_out: float32 [64, 128, 256], P('len', 'hgt')
- enthalpy_out: float32 [4096, 128], P(('len', 'hgt'))
Inputs may be any that keep to these rules, and one draw needn't show every extreme that they name: Rows 0 to pair_rows[s, d] - 1 of pair (s, d) are live, the others are padding. In every draw one owner receives 256 live rows from every air device; other owners receive fewer.
All inputs are finite; a program needn't handle non-finite values. No bound on the sum of `fluid` on one device may be relied on, other than what follows from the above.
Results may differ from a plain program's by a relative error of at most 0.0003.
Values sent between devices are 32-bit elements; how exact they have to be, the bound alone decides.
No kernel may reach another device: no remote copies, remote signals or barrier semaphores. Data moves between devices by JAX's collectives and lax.ppermute only.
A program may use at most 64 MiB of HBM per device.

v0:
```python
import jax
import jax.numpy as jnp
from jax import lax
from jax.sharding import PartitionSpec as P

LATENT = 1.0
SOLID_SLOPE = 2.0
DT_AIR = 0.1
DT_NODE = 0.05


def with_halo(cells, sides, width):
    for axis, dim in sides:
        count = lax.axis_size(axis)
        ends = count - 1
        head = lax.slice_in_dim(cells, 0, width, axis=dim)
        tail = lax.slice_in_dim(cells, cells.shape[dim] - width, cells.shape[dim], axis=dim)
        cells = jnp.concatenate(
            [
                lax.ppermute(tail, axis, [(i, (i + 1) % count) for i in range(ends)]),
                cells,
                lax.ppermute(head, axis, [((i + 1) % count, i) for i in range(ends)]),
            ],
            axis=dim,
        )
    return cells


def warmth_per_point(matrix_coefficients):
    return jnp.where(
        matrix_coefficients < 0.0,
        SOLID_SLOPE * matrix_coefficients,
        jnp.where(matrix_coefficients > LATENT, matrix_coefficients - LATENT, 0.0),
    )


def local(
    air_temp, velocity, fluid, enthalpy, adjacency_lists, send_cells, contact, pair_rows, recv_nodes
):
    pair_len = send_cells.shape[2]
    cell_index = send_cells[0]
    index_of_node = recv_nodes[0]
    live_rows = jnp.arange(pair_len)[None, :] < pair_rows[0][:, None]
    weight = jnp.where(live_rows, contact[0], jnp.float32(0.0))
    fluid_f = fluid.astype(jnp.float32)
    slow_up = jnp.maximum(velocity, 0.0)
    slow_down = jnp.minimum(velocity, 0.0)
    temper = air_temp
    heat_content_sum = enthalpy
    for repeat in range(2):
        cell_flat = temper.reshape(-1)
        sampled = cell_flat[cell_index]
        outgoing = jnp.stack([sampled, weight], axis=1)
        meat_point_warmth = warmth_per_point(heat_content_sum)
        linear_point_list = meat_point_warmth.reshape(-1)
        surface_boundary = linear_point_list[index_of_node]
        incoming = lax.all_to_all(outgoing, ("len", "hgt"), split_axis=0, concat_axis=0, tiled=True)
        returned = lax.all_to_all(
            surface_boundary, ("len", "hgt"), split_axis=0, concat_axis=0, tiled=True
        )
        flux_row = incoming[:, 1] * (incoming[:, 0] - surface_boundary)
        node_flux = jax.ops.segment_sum(
            flux_row.reshape(-1), index_of_node.reshape(-1), num_segments=linear_point_list.shape[0]
        )
        collected_neighbour_data = jnp.take_along_axis(
            jnp.broadcast_to(meat_point_warmth[:, None, :], adjacency_lists.shape),
            adjacency_lists,
            axis=2,
        )
        diffusive_flux = jnp.sum(collected_neighbour_data - meat_point_warmth[:, None, :], axis=1)
        heat_content_sum = heat_content_sum + DT_NODE * (
            diffusive_flux + node_flux.reshape(heat_content_sum.shape)
        )
        src_row = weight * (returned - sampled)
        source = jax.ops.segment_sum(
            src_row.reshape(-1), cell_index.reshape(-1), num_segments=cell_flat.shape[0]
        ).reshape(temper.shape)
        padded = with_halo(temper, (("len", 0), ("hgt", 1)), 1)
        behind = padded[:-2, 1:-1]
        ahead = padded[2:, 1:-1]
        zero_column = jnp.zeros_like(temper[:, :, :1])
        left_cell = jnp.concatenate([zero_column, temper[:, :, :-1]], axis=2)
        right_cell = jnp.concatenate([temper[:, :, 1:], zero_column], axis=2)
        laplace = ahead + behind + padded[1:-1, 2:] + padded[1:-1, :-2]
        laplace = laplace + right_cell + left_cell - 6.0 * temper
        advect = slow_up * (temper - behind) + slow_down * (ahead - temper)
        temper = temper + fluid_f * DT_AIR * (laplace - advect + source)
    return (temper, heat_content_sum)


def solution(mesh):
    in_specs = (
        P("len", "hgt", None),
        P("len", "hgt", None),
        P("len", "hgt", None),
        P(("len", "hgt"), None),
        P(("len", "hgt"), None, None),
        P(("len", "hgt"), None, None),
        P(("len", "hgt"), None, None),
        P(("len", "hgt"), None),
        P(("len", "hgt"), None, None),
    )
    out_specs = (P("len", "hgt", None), P(("len", "hgt"), None))
    return jax.shard_map(local, mesh=mesh, in_specs=in_specs, out_specs=out_specs, check_vma=False)
```

profile of v0, /device:TPU:1, one launch (start us, length us, event | category | flops | bytes accessed | tf_op | source)
XLA Modules:
  0.0 2156.6 jit_solution(16347928293359081255)
XLA Ops:
  0.6 0.9 fusion
  1.6 0.1 copy.13
  1.7 0.6 copy-done.7
  2.3 320.1 %gather_fusion = f32[32768]{0:T(1024)} fusion(f32[4096]{0:T(1024)S(1)} %get-tuple-element.24, s32[32768]{0:T(1024)S(1)} %broadcast_clamp_fusion.1), kind=kCustom, calls=%fused_computation.2 | custom fusion | bytes 393216 | tf_op jit(solution)/shard_map/gather | solution.py:56
  322.3 11.5 all-to-all-start
  333.9 3.5 collective-permute-start.1
  337.4 1.9 collective-permute-start
  339.3 0.1 fusion.55
  339.5 0.1 copy.15
  339.6 0.8 copy-done.1
  340.4 190.9 %gather_fusion.4 = f32[32768]{0:T(1024)S(1)} fusion(f32[32,8,128]{2,1,0:T(8,128)S(1)} %broadcast_in_dim.17, s32[32768]{0:T(1024)S(1)} %fusion.6), kind=kCustom, calls=%fused_computation.clone | custom fusion | bytes 655360 | tf_op jit(solution)/shard_map/jit(take_along_axis)/gather | solution.py:65
  531.4 0.7 fusion.5
  532.0 0.2 copy-done.2
  532.3 0.2 compare_select_fusion
  532.5 0.1 iota_compare_fusion
  532.7 0.1 copy.12
  532.7 0.1 copy.11
  532.8 0.7 copy-done.4
  533.6 0.1 copy.16
  533.6 180.5 %gather_fusion.1 = f32[32768]{0:T(1024)S(1)} fusion(f32[16384]{0:T(1024)S(1)} %bitcast.71, s32[32768]{0:T(1024)S(1)} %broadcast_clamp_fusion), kind=kCustom, calls=%fused_computation.3 | custom fusion | bytes 393216 | tf_op jit(solution)/shard_map/gather | solution.py:52
  714.3 1.3 collective-permute-start.2
  715.6 4.0 collective-permute-start.3
  719.6 171.1 %scatter_custom_fusion = f32[16384]{0:T(1024)S(1)} fusion(s32[32768]{0:T(1024)S(1)} %bitcast.90, f32[32768]{0:T(1024)S(1)} %subtract_multiply_fusion.3, f32[]{:T(128)} %constant.19.clone.1), kind=kCustom, calls=%fused_computation.80 | custom fusion | flops 32768 | bytes 65540 | tf_op jit(solution)/shard_map/scatter-add | solution.py:75
  890.8 0.1 fusion.29
  890.9 180.5 %gather_fusion.3 = f32[32768]{0:T(1024)S(1)} fusion(f32[16384]{0:T(1024)S(1)} %bitcast.72, s32[32768]{0:T(1024)S(1)} %broadcast_clamp_fusion), kind=kCustom, calls=%fused_computation.5 | custom fusion | bytes 393216 | tf_op jit(solution)/shard_map/gather | solution.py:52
  1071.5 1.1 pad_maximum_fusion
  1072.6 12.5 all-to-all-start.1
  1085.1 3.0 collective-permute-start.4
  1088.1 2.6 collective-permute-start.5
  1090.7 0.1 fusion.53
  1090.8 0.7 collective-permute-done.5
  1091.5 1.3 collective-permute-start.6
  1092.8 4.1 collective-permute-start.7
  1096.9 13.2 all-to-all-start.3
  1110.1 0.2 fusion.51
  1110.3 0.9 subtract_multiply_fusion.2
  1111.2 171.0 %scatter_custom_fusion.1 = f32[4096]{0:T(1024)S(1)} fusion(s32[32768]{0:T(1024)S(1)} %bitcast.92, f32[32768]{0:T(1024)S(1)} %subtract_multiply_fusion.2, f32[]{:T(128)} %constant.19.clone.1), kind=kCustom, calls=%fused_computation.95 | custom fusion | flops 32768 | bytes 16388 | tf_op jit(solution)/shard_map/scatter-add | solution.py:62
  1282.3 319.6 %gather_fusion.2 = f32[32768]{0:T(1024)} fusion(f32[4096]{0:T(1024)S(1)} %bitcast.70, s32[32768]{0:T(1024)S(1)} %broadcast_clamp_fusion.1), kind=kCustom, calls=%fused_computation.4 | custom fusion | bytes 393216 | tf_op jit(solution)/shard_map/gather | solution.py:56
  1601.9 0.2 fusion.50
  1602.1 0.9 subtract_multiply_fusion
  1603.0 171.0 %scatter_custom_fusion.3 = f32[4096]{0:T(1024)S(1)} fusion(s32[32768]{0:T(1024)S(1)} %bitcast.93, f32[32768]{0:T(1024)S(1)} %subtract_multiply_fusion, f32[]{:T(128)} %constant.19.clone.1), kind=kCustom, calls=%fused_computation.93 | custom fusion | flops 32768 | bytes 16388 | tf_op jit(solution)/shard_map/scatter-add | solution.py:62
  1774.1 190.9 %gather_fusion.5 = f32[32768]{0:T(1024)S(1)} fusion(f32[32,8,128]{2,1,0:T(8,128)S(1)} %broadcast_in_dim.19, s32[32768]{0:T(1024)S(1)} %fusion.6), kind=kCustom, calls=%fused_computation.1.clone | custom fusion | bytes 655360 | tf_op jit(solution)/shard_map/jit(take_along_axis)/gather | solution.py:65
  1965.0 9.8 all-to-all-start.2
  1974.8 0.1 fusion.3
  1974.9 0.6 fusion.42
  1975.5 9.2 all-to-all-done.2
  1984.8 171.1 %scatter_custom_fusion.2 = f32[16384]{0:T(1024)S(1)} fusion(s32[32768]{0:T(1024)S(1)} %bitcast.91, f32[32768]{0:T(1024)S(1)} %subtract_multiply_fusion.1, f32[]{:T(128)} %constant.19.clone.1), kind=kCustom, calls=%fused_computation.78 | custom fusion | flops 32768 | bytes 65540 | tf_op jit(solution)/shard_map/scatter-add | solution.py:75
  2155.9 0.7 fusion.14
  (50 shorter events, 0.5 us)
Async XLA Ops:
  1.6 0.7 copy-start.7
  322.3 11.5 copy-start
  322.3 17.1 copy-start.3
  322.3 397.2 %all-to-all-start = ((f32[128,1,256]{2,1,0:T(1,128)}), f32[128,1,256]{2,1,0:T(1,128)S(1)}, u32[]{:S(2)}, u32[]{:S(2)}) async-start(f32[128,1,256]{2,1,0:T(1,128)} %bitcast.3), calls=%async_computation | async-start | bytes 262144 | tf_op jit(solution)/shard_map/all_to_all | solution.py:58
  333.9 380.3 %collective-permute-start.1 = (f32[1,8,256]{2,1,0:T(8,128)S(1)}, f32[1,8,256]{2,1,0:T(8,128)S(1)}, u32[]{:S(2)}, u32[]{:S(2)}) collective-permute-start(f32[1,8,256]{2,1,0:T(8,128)S(1)} %get-tuple-element.22), channel_id=1, source_target_pairs={{0,16},{16,32},{32,48},{48,64},{64,80},{80,96},{96,112},{1,17},{17... | collective-permute-start | bytes 24584 | tf_op jit(solution)/shard_map/ppermute | solution.py:20
  337.4 376.8 %collective-permute-start = (f32[1,8,256]{2,1,0:T(8,128)S(1)}, f32[1,8,256]{2,1,0:T(8,128)S(1)}, u32[]{:S(2)}, u32[]{:S(2)}) collective-permute-start(f32[1,8,256]{2,1,0:T(8,128)S(1)} %get-tuple-element.21), channel_id=1, source_target_pairs={{16,0},{32,16},{48,32},{64,48},{80,64},{96,80},{112,96},{17,1},{33... | collective-permute-start | bytes 24584 | tf_op jit(solution)/shard_map/ppermute | solution.py:22
  339.5 0.9 copy-start.1
  531.4 0.9 copy-start.2
  531.4 0.9 copy-start.10
  532.7 0.9 copy-start.4
  714.3 176.5 %collective-permute-start.2 = (f32[10,1,256]{2,1,0:T(1,128)S(1)}, f32[10,1,256]{2,1,0:T(1,128)S(1)}, u32[]{:S(2)}, u32[]{:S(2)}) collective-permute-start(f32[10,1,256]{2,1,0:T(1,128)S(1)} %get-tuple-element.13), channel_id=1, source_target_pairs={{1,0},{2,1},{3,2},{4,3},{5,4},{6,5},{7,6},{8,7},{9,8},{10,9},{11,1... | collective-permute-start | bytes 30728 | tf_op jit(solution)/shard_map/ppermute | solution.py:22
  715.6 175.2 %collective-permute-start.3 = (f32[10,1,256]{2,1,0:T(1,128)S(1)}, f32[10,1,256]{2,1,0:T(1,128)S(1)}, u32[]{:S(2)}, u32[]{:S(2)}) collective-permute-start(f32[10,1,256]{2,1,0:T(1,128)S(1)} %get-tuple-element.14), channel_id=1, source_target_pairs={{0,1},{1,2},{2,3},{3,4},{4,5},{5,6},{6,7},{7,8},{8,9},{9,10},{10,1... | collective-permute-start | bytes 30728 | tf_op jit(solution)/shard_map/ppermute | solution.py:20
  719.6 171.2 %copy-start.5 = (s32[8,8,256]{2,1,0:T(8,128)S(1)}, s32[8,8,256]{2,1,0:T(8,128)}, u32[]{:S(2)}) copy-start(s32[8,8,256]{2,1,0:T(8,128)} %param.13) | copy-start | bytes 196612
  719.6 171.2 %copy-start.6 = (f32[8,8,256]{2,1,0:T(8,128)S(1)}, f32[8,8,256]{2,1,0:T(8,128)}, u32[]{:S(2)}) copy-start(f32[8,8,256]{2,1,0:T(8,128)} %param.12) | copy-start | bytes 196612
  1072.6 24.2 %all-to-all-start.1 = ((f32[128,2,256]{2,1,0:T(2,128)}), f32[128,2,256]{2,1,0:T(2,128)S(1)}, u32[]{:S(2)}, u32[]{:S(2)}) async-start(f32[128,2,256]{2,1,0:T(2,128)} %get-tuple-element.10), calls=%async_computation.1 | async-start | bytes 524288 | tf_op jit(solution)/shard_map/all_to_all | solution.py:57
  1085.1 5.7 collective-permute-start.4
  1088.1 3.4 collective-permute-start.5
  1091.5 1064.4 %collective-permute-start.6 = (f32[10,1,256]{2,1,0:T(1,128)S(1)}, f32[10,1,256]{2,1,0:T(1,128)S(1)}, u32[]{:S(2)}, u32[]{:S(2)}) collective-permute-start(f32[10,1,256]{2,1,0:T(1,128)S(1)} %get-tuple-element.11), channel_id=1, source_target_pairs={{1,0},{2,1},{3,2},{4,3},{5,4},{6,5},{7,6},{8,7},{9,8},{10,9},{11,1... | collective-permute-start | bytes 30728 | tf_op jit(solution)/shard_map/ppermute | solution.py:22
  1092.8 1063.1 %collective-permute-start.7 = (f32[10,1,256]{2,1,0:T(1,128)S(1)}, f32[10,1,256]{2,1,0:T(1,128)S(1)}, u32[]{:S(2)}, u32[]{:S(2)}) collective-permute-start(f32[10,1,256]{2,1,0:T(1,128)S(1)} %get-tuple-element.12), channel_id=1, source_target_pairs={{0,1},{1,2},{2,3},{3,4},{4,5},{5,6},{6,7},{7,8},{8,9},{9,10},{10,1... | collective-permute-start | bytes 30728 | tf_op jit(solution)/shard_map/ppermute | solution.py:20
  1096.9 505.0 %all-to-all-start.3 = ((f32[128,2,256]{2,1,0:T(2,128)}), f32[128,2,256]{2,1,0:T(2,128)S(1)}, u32[]{:S(2)}, u32[]{:S(2)}) async-start(f32[128,2,256]{2,1,0:T(2,128)} %get-tuple-element.9), calls=%async_computation.3 | async-start | bytes 524288 | tf_op jit(solution)/shard_map/all_to_all | solution.py:57
  1110.3 172.0 %copy-start.8 = (f32[32,128]{1,0:T(8,128)S(1)}, f32[32,128]{1,0:T(8,128)}, u32[]{:S(2)}) copy-start(f32[32,128]{1,0:T(8,128)} %param.14) | copy-start | bytes 49156
  1965.0 9.8 copy-start.9
  1965.0 19.7 all-to-all-start.2
where the time goes:
time: 2160 us
  local copies, waits for them, and re-layouts  1390 us (64%)
  other arithmetic  691 us (32%)
  starting transfers between devices  68.7 us (3%)
    gather x2, local copies, waits for them, and re-layouts, local(): surface_boundary = linear_point_list[index_of_node]  640 us
    gather x2, local copies, waits for them, and re-layouts, local(): jnp.take_along_axis(jnp.broadcast_to(meat_point_warmth[:, None, :], adjac...  382 us
    gather x2, local copies, waits for them, and re-layouts, local(): sampled = cell_flat[cell_index]  361 us
    scatter-add x2, other arithmetic, local(): jax.ops.segment_sum(src_row.reshape(-1), cell_index.reshape(-1), num_segm...  342 us
    scatter-add x2, other arithmetic, local(): jax.ops.segment_sum(flux_row.reshape(-1), index_of_node.reshape(-1), num_...  342 us
  transfers between devices with their start and end apart: 12, of which 2 were waited for; matrix products, arithmetic and copies ran while one was open for 73% of the time, Pallas kernels for 0%

commit v1 on v0

v1 whole, which is shorter than its diff:
```python
import jax
import jax.numpy as jnp
from jax import lax
from jax.experimental import pallas as pl
from jax.experimental.pallas import tpu as pltpu
from jax.sharding import PartitionSpec as P

LATENT = 1.0
SOLID_SLOPE = 2.0
DT_AIR = 0.1
DT_NODE = 0.05

F32 = jnp.float32
BF16 = jnp.bfloat16
I32 = jnp.int32
LANES = 128
PAIRS = 128
PAIR_ROWS = 256
GROUP = 16


def node_temp(enthalpy):
    return jnp.where(
        enthalpy < 0.0,
        SOLID_SLOPE * enthalpy,
        jnp.where(enthalpy > LATENT, enthalpy - LATENT, 0.0),
    )


def take(row, lane):
    return jnp.take_along_axis(jnp.broadcast_to(row, lane.shape), lane, axis=1)


def gather(rows, index):
    lane = index & (LANES - 1)
    high = index >> 7
    parts = [jnp.zeros(index.shape, F32) for _ in range(4)]
    for j, row in enumerate(rows):
        parts[j % 4] = jnp.where(high == j, take(row, lane), parts[j % 4])
    return (parts[0] + parts[1]) + (parts[2] + parts[3])


def air_rows(air_ref):
    return [
        air_ref[i, j : j + 1, h : h + LANES]
        for i in range(8)
        for j in range(8)
        for h in (0, LANES)
    ]


def iota16():
    return lax.broadcasted_iota(I32, (16, LANES), 0).astype(F32).astype(BF16)


def as_bf16(index):
    return index.astype(F32).astype(BF16)


def two_parts(value):
    top = value.astype(BF16)
    return top, (value - top.astype(F32)).astype(BF16)


def one_hot(index, count, iota):
    one = jnp.ones((16, LANES), BF16)
    zero = jnp.zeros((16, LANES), BF16)
    return jnp.concatenate(
        [jnp.where(index == iota + BF16(16 * i), one, zero) for i in range(count // 16)], axis=0
    )


def weighted(index, values, count, iota):
    zero = jnp.zeros((16, LANES), BF16)
    masks = [index == iota + BF16(16 * i) for i in range(count // 16)]
    return jnp.concatenate(
        [jnp.where(m, part, zero) for v in values for part in two_parts(v) for m in masks], axis=0
    )


def scatter(split, values, high_count, n_values, pairs=PAIRS, group=GROUP):
    iota = iota16()

    def body(g, acc):
        left, right = [], []
        for k in range(group):
            pair = (pl.multiple_of(g * group, group), k)
            for half in range(2):
                high, low = split(pair, half)
                left.append(weighted(as_bf16(high), values(pair, half), high_count, iota))
                right.append(one_hot(as_bf16(low), LANES, iota))
        left = jnp.concatenate(left, axis=1)
        right = jnp.concatenate(right, axis=1)
        return acc + lax.dot_general(
            left, right, (((1,), (1,)), ((), ())), preferred_element_type=F32
        )

    acc = lax.fori_loop(
        0, pairs // group, body, jnp.zeros((2 * n_values * high_count, LANES), F32)
    )
    out = []
    for n in range(n_values):
        at = 2 * n * high_count
        out.append(acc[at : at + high_count] + acc[at + high_count : at + 2 * high_count])
    return out


def lane_row(ref, row):
    return jnp.broadcast_to(ref[pl.ds(row, 1), :], (16, LANES))


def pair_row(ref, pair, half):
    start, k = pair
    view = ref.at[pl.ds(start, GROUP), half * LANES : (half + 1) * LANES]
    return jnp.broadcast_to(view[k : k + 1, :], (16, LANES))


def cell_split(cell_ref):
    def split(pair, half):
        cell = pair_row(cell_ref, pair, half)
        return ((cell >> 7) & 1) * 64 + (cell >> 8), cell & (LANES - 1)

    return split


def node_split(node_ref):
    def split(pair, half):
        node = pair_row(node_ref, pair, half)
        return node >> 7, node & (LANES - 1)

    return split


def to_block(table):
    return jnp.concatenate([table[:64], table[64:]], axis=1).reshape(8, 8, 256)


def pre_kernel(air_ref, enthalpy_ref, cell_ref, contact_ref, rows_ref, node_ref, out_ref, weight_ref):
    live = jnp.transpose(jnp.broadcast_to(rows_ref[...], (LANES, LANES)))
    for half in range(2):
        at = half * LANES
        spot = lax.broadcasted_iota(I32, (PAIRS, LANES), 1) + at
        weight_ref[:, at : at + LANES] = jnp.where(
            spot < live, contact_ref[:, at : at + LANES], 0.0
        )
    pack(air_ref, node_temp(enthalpy_ref[...]), cell_ref, weight_ref, node_ref, out_ref, True)


def pack(air_ref, warmth, cell_ref, weight_ref, node_ref, out_ref, with_weight):
    per_pair = 6 if with_weight else 4
    warm_rows = [warmth[j : j + 1] for j in range(warmth.shape[0])]
    table = air_rows(air_ref)

    def body(k, carry):
        at = pl.ds(pl.multiple_of(k * 8, 8), 8)
        for half in range(2):
            lanes = slice(half * LANES, (half + 1) * LANES)
            weight = weight_ref[at, lanes]
            base = k * 8 * per_pair + half
            out_ref[pl.ds(base, 8, stride=per_pair), :] = weight * gather(table, cell_ref[at, lanes])
            out_ref[pl.ds(base + 2, 8, stride=per_pair), :] = gather(warm_rows, node_ref[at, lanes])
            if with_weight:
                out_ref[pl.ds(base + 4, 8, stride=per_pair), :] = weight
        return carry

    lax.fori_loop(0, PAIRS // 8, body, 0)


def side_kernel(cell_ref, weight_ref, out_ref):
    (total,) = scatter(
        cell_split(cell_ref), lambda p, h: [pair_row(weight_ref, p, h)], 128, 1
    )
    out_ref[...] = to_block(total)


def conduction(warmth, links_ref):
    rows = []
    for b in range(warmth.shape[0]):
        linked = take(warmth[b : b + 1], links_ref[b])
        rows.append(jnp.sum(linked, axis=0, keepdims=True))
    return jnp.concatenate(rows, axis=0) - 8.0 * warmth


def air_step(air, velocity, fluid, behind_halo, ahead_halo, left_halo, right_halo, source):
    behind = jnp.concatenate([behind_halo, air[:-1]], axis=0)
    ahead = jnp.concatenate([air[1:], ahead_halo], axis=0)
    row = lax.broadcasted_iota(I32, air.shape, 1)
    lane = lax.broadcasted_iota(I32, air.shape, 2)
    low = jnp.where(row == 0, left_halo, pltpu.roll(air, 1, 1))
    high = jnp.where(row == 7, right_halo, pltpu.roll(air, 7, 1))
    flat = air.reshape(64, 256)
    left = jnp.where(lane == 0, 0.0, pltpu.roll(flat, 1, 1).reshape(air.shape))
    right = jnp.where(lane == 255, 0.0, pltpu.roll(flat, 255, 1).reshape(air.shape))
    laplace = (ahead + behind) + (high + low) + (right + left) - 6.0 * air
    advect = jnp.maximum(velocity, 0.0) * (air - behind) + jnp.minimum(velocity, 0.0) * (
        ahead - air
    )
    return air + fluid.astype(F32) * DT_AIR * (laplace - advect + source)


def step(
    received_ref, per_pair, air_ref, velocity_ref, fluid_ref, enthalpy_ref, links_ref, cell_ref,
    weight_ref, node_ref, behind_ref, ahead_ref, left_ref, right_ref, cell_total, node_total,
    air_out_ref, enthalpy_out_ref,
):
    def node_values(p, h):
        base = (p[0] + p[1]) * per_pair + h
        values = [lane_row(received_ref, base)]
        if node_total is None:
            values.append(lane_row(received_ref, base + 4))
        return values

    sums = scatter(node_split(node_ref), node_values, 32, 2 if node_total is None else 1)
    if node_total is None:
        node_total = sums[1]
    enthalpy = enthalpy_ref[...]
    warmth = node_temp(enthalpy)
    enthalpy_out_ref[...] = enthalpy + DT_NODE * (
        conduction(warmth, links_ref) + (sums[0] - warmth * node_total)
    )
    (heat,) = scatter(
        cell_split(cell_ref),
        lambda p, h: [pair_row(weight_ref, p, h) * lane_row(received_ref, (p[0] + p[1]) * per_pair + 2 + h)],
        128,
        1,
    )
    air = air_ref[...]
    air_out_ref[...] = air_step(
        air, velocity_ref[...], fluid_ref[...], behind_ref[...], ahead_ref[...], left_ref[...],
        right_ref[...], to_block(heat) - air * cell_total,
    )
    return node_total


def mid_kernel(
    received_ref, air_ref, velocity_ref, fluid_ref, enthalpy_ref, links_ref, cell_ref, weight_ref,
    node_ref, cell_total_ref, behind_ref, ahead_ref, left_ref, right_ref,
    air_out_ref, enthalpy_out_ref, node_total_ref, out_ref,
):
    node_total_ref[...] = step(
        received_ref, 6, air_ref, velocity_ref, fluid_ref, enthalpy_ref, links_ref, cell_ref,
        weight_ref, node_ref, behind_ref, ahead_ref, left_ref, right_ref, cell_total_ref[...], None,
        air_out_ref, enthalpy_out_ref,
    )
    pack(
        air_out_ref, node_temp(enthalpy_out_ref[...]), cell_ref, weight_ref, node_ref, out_ref, False
    )


def post_kernel(
    received_ref, air_ref, velocity_ref, fluid_ref, enthalpy_ref, links_ref, cell_ref, weight_ref,
    node_ref, cell_total_ref, node_total_ref, behind_ref, ahead_ref, left_ref, right_ref,
    air_out_ref, enthalpy_out_ref,
):
    step(
        received_ref, 4, air_ref, velocity_ref, fluid_ref, enthalpy_ref, links_ref, cell_ref,
        weight_ref, node_ref, behind_ref, ahead_ref, left_ref, right_ref, cell_total_ref[...],
        node_total_ref[...], air_out_ref, enthalpy_out_ref,
    )


def call(kernel, name, shapes):
    return pl.pallas_call(
        kernel,
        out_shape=[jax.ShapeDtypeStruct(s, F32) for s in shapes],
        name=name,
        compiler_params=pltpu.CompilerParams(vmem_limit_bytes=32 * 1024 * 1024),
    )


def halos(air):
    out = []
    for axis, dim in (("len", 0), ("hgt", 1)):
        count = lax.axis_size(axis)
        head = lax.slice_in_dim(air, 0, 1, axis=dim)
        tail = lax.slice_in_dim(air, air.shape[dim] - 1, air.shape[dim], axis=dim)
        out.append(lax.ppermute(tail, axis, [(i, i + 1) for i in range(count - 1)]))
        out.append(lax.ppermute(head, axis, [(i + 1, i) for i in range(count - 1)]))
    return out


def exchange(packed):
    both = packed.reshape(PAIRS, 1, -1)
    both = lax.all_to_all(both, ("len", "hgt"), split_axis=0, concat_axis=0, tiled=True)
    return both.reshape(packed.shape)


def local(
    air_temp, velocity, fluid, enthalpy, adjacency_lists, send_cells, contact, pair_rows, recv_nodes
):
    cells, nodes = send_cells[0], recv_nodes[0]
    block, panel, pairs = air_temp.shape, enthalpy.shape, cells.shape
    packed, weight = call(pre_kernel, "pack_first", [(6 * PAIRS, LANES), pairs])(
        air_temp, enthalpy, cells, contact[0], pair_rows, nodes
    )
    received = exchange(packed)
    edges = halos(air_temp)
    (cell_total,) = call(side_kernel, "cell_totals", [block])(cells, weight)
    air, heat, node_total, packed = call(
        mid_kernel, "first_step", [block, panel, panel, (4 * PAIRS, LANES)]
    )(
        received, air_temp, velocity, fluid, enthalpy, adjacency_lists, cells, weight, nodes,
        cell_total, *edges,
    )
    received = exchange(packed)
    edges = halos(air)
    air, heat = call(post_kernel, "second_step", [block, panel])(
        received, air, velocity, fluid, heat, adjacency_lists, cells, weight, nodes, cell_total,
        node_total, *edges,
    )
    return air, heat


def solution(mesh):
    rows = P(("len", "hgt"), None)
    lists = P(("len", "hgt"), None, None)
    grid = P("len", "hgt", None)
    in_specs = (grid, grid, grid, rows, lists, lists, lists, rows, lists)
    return jax.shard_map(
        local, mesh=mesh, in_specs=in_specs, out_specs=(grid, rows), check_vma=False
    )
```

time: 2160 us -> 95.2 us (0.04)
  the two profiles are of different devices: /device:TPU:1 before, /device:TPU:30 now
where the time goes in v1:
time: 95.2 us; the launch traced here: 94.7 us
  starting transfers between devices  44.6 us (47%)
  Pallas kernels  41.4 us (43%)
  local copies, waits for them, and re-layouts  4.98 us (5%)
  waiting for transfers between devices  2.82 us (3%)
    all_to_all x2, starting transfers between devices, exchange(): lax.all_to_all(both, ('len', 'hgt'), split_axis=0, concat_axis=0, tiled=T...  20.8 us
    pallas_call x1, Pallas kernels, local(): call(mid_kernel, 'first_step', [block, panel, panel, (4 * PAIRS, LANES)])  17.2 us
    ppermute x4, starting transfers between devices, halos(): out.append(lax.ppermute(head, axis, [(i + 1, i) for i in range(count - 1)]))  15.7 us
    pallas_call x1, Pallas kernels, local(): call(post_kernel, 'second_step', [block, panel])  10.6 us
    ppermute x4, starting transfers between devices, halos(): out.append(lax.ppermute(tail, axis, [(i, i + 1) for i in range(count - 1)]))  8.14 us
    pallas_call x1, Pallas kernels, local(): call(pre_kernel, 'pack_first', [(6 * PAIRS, LANES), pairs])  7.74 us
    pallas_call x1, Pallas kernels, local(): cell_total, = call(side_kernel, 'cell_totals', [block])(cells, weight)  5.74 us
    unnamed x26, local copies, waits for them, and re-layouts  4.95 us
  transfers between devices with their start and end apart: 10, of which 2 were waited for; matrix products, arithmetic and copies ran while one was open for 0% of the time, Pallas kernels for 6%

profile of v1, /device:TPU:30, one launch (start us, length us, event | category | flops | bytes accessed | tf_op | source)
XLA Modules:
  0.0 94.7 jit_solution(5638178080831624837)
XLA Ops:
  0.6 0.0 copy-start.12
  0.6 0.6 copy-done.12
  1.3 0.0 copy-start
  1.3 0.9 copy-done
  2.2 0.0 copy-start.2
  2.2 0.9 copy-done.2
  3.1 0.0 copy-start.5
  3.1 0.8 copy-done.5
  3.9 0.0 copy-start.9
  3.9 0.9 copy-done.9
  4.8 0.0 copy-start.10
  4.8 0.7 copy-done.10
  5.6 7.7 %pack_first.1 = (f32[768,128]{1,0:T(8,128)}, f32[128,256]{1,0:T(8,128)S(1)}) custom-call(f32[8,8,256]{2,1,0:T(8,128)S(1)} %copy-done.5, f32[32,128]{1,0:T(8,128)S(1)} %copy-done.10, s32[128,256]{1,0:T(8,128)S(1)} %bitcast.7, f32[128,256]{1,0:T(8,128)S(1)} %bitcast.16, s32[1,128]{1,0:T(1,128)S(1)} %copy-done.12, s32[128,256]{1,0:T(8,128)S(1)} %bitcast.12), custom_call_target="tpu_custom_call" | custom-call | tf_op jit(solution)/shard_map/pack_first/pallas_call | solution.py:293
  13.3 0.0 copy-start.6
  13.3 10.2 %all-to-all-start = ((f32[128,1,768]{2,1,0:T(1,128)}), f32[128,1,768]{2,1,0:T(1,128)S(1)}, u32[]{:S(2)}, u32[]{:S(2)}) async-start(f32[128,1,768]{2,1,0:T(1,128)} %bitcast.3), calls=%async_computation | async-start | bytes 786432 | tf_op jit(solution)/shard_map/all_to_all | solution.py:284
  23.6 0.0 copy-done.6
  23.6 0.0 copy-start.8
  23.6 5.7 %collective-permute-start.3 = (f32[8,1,256]{2,1,0:T(1,128)S(1)}, f32[8,1,256]{2,1,0:T(1,128)S(1)}, u32[]{:S(2)}, u32[]{:S(2)}) collective-permute-start(f32[8,1,256]{2,1,0:T(1,128)S(1)} %get-tuple-element.18), channel_id=1, source_target_pairs={{1,0},{2,1},{3,2},{4,3},{5,4},{6,5},{7,6},{8,7},{9,8},{10,9},{11,1... | collective-permute-start | bytes 24584 | tf_op jit(solution)/shard_map/ppermute | solution.py:278
  29.3 1.9 %collective-permute-start.2 = (f32[8,1,256]{2,1,0:T(1,128)S(1)}, f32[8,1,256]{2,1,0:T(1,128)S(1)}, u32[]{:S(2)}, u32[]{:S(2)}) collective-permute-start(f32[8,1,256]{2,1,0:T(1,128)S(1)} %get-tuple-element.19), channel_id=1, source_target_pairs={{0,1},{1,2},{2,3},{3,4},{4,5},{5,6},{6,7},{7,8},{8,9},{9,10},{10,1... | collective-permute-start | bytes 24584 | tf_op jit(solution)/shard_map/ppermute | solution.py:277
  31.2 2.2 %collective-permute-start.1 = (f32[1,8,256]{2,1,0:T(8,128)S(1)}, f32[1,8,256]{2,1,0:T(8,128)S(1)}, u32[]{:S(2)}, u32[]{:S(2)}) collective-permute-start(f32[1,8,256]{2,1,0:T(8,128)S(1)} %get-tuple-element.20), channel_id=1, source_target_pairs={{16,0},{32,16},{48,32},{64,48},{80,64},{96,80},{112,96},{17,1},{33... | collective-permute-start | bytes 24584 | tf_op jit(solution)/shard_map/ppermute | solution.py:278
  33.4 2.2 %collective-permute-start = (f32[1,8,256]{2,1,0:T(8,128)S(1)}, f32[1,8,256]{2,1,0:T(8,128)S(1)}, u32[]{:S(2)}, u32[]{:S(2)}) collective-permute-start(f32[1,8,256]{2,1,0:T(8,128)S(1)} %get-tuple-element.21), channel_id=1, source_target_pairs={{0,16},{16,32},{32,48},{48,64},{64,80},{80,96},{96,112},{1,17},{17... | collective-permute-start | bytes 24584 | tf_op jit(solution)/shard_map/ppermute | solution.py:277
  35.5 0.0 copy-done.1
  35.6 0.0 copy-start.3
  35.6 0.0 copy-start.4
  35.6 0.0 copy-start.7
  35.6 5.7 %cell_totals.1.cell_total_ref = f32[8,8,256]{2,1,0:T(8,128)S(1)} custom-call(s32[128,256]{1,0:T(8,128)S(1)} %bitcast.8, f32[128,256]{1,0:T(8,128)S(1)} %get-tuple-element.9.weight_ref), custom_call_target="tpu_custom_call" | custom-call | tf_op jit(solution)/shard_map/cell_totals/pallas_call | solution.py:298
  41.3 0.0 collective-permute-done.3.right_ref
  41.4 0.0 collective-permute-done.2.left_ref
  41.4 0.0 collective-permute-done.1.ahead_ref
  41.4 0.0 collective-permute-done.behind_ref
  41.4 0.0 all-to-all-done
  41.4 0.0 copy-done.11
  41.4 0.0 copy-done.8
  41.4 0.0 copy-done.3
  41.4 0.0 copy-done.4
  41.4 0.0 copy-done.7
  41.4 17.2 %first_step.1 = (f32[8,8,256]{2,1,0:T(8,128)S(1)}, f32[32,128]{1,0:T(8,128)S(1)}, f32[32,128]{1,0:T(8,128)S(1)}, f32[512,128]{1,0:T(8,128)}) custom-call(f32[768,128]{1,0:T(8,128)S(1)} %bitcast.11, f32[8,8,256]{2,1,0:T(8,128)S(1)} %copy-done.6, f32[8,8,256]{2,1,0:T(8,128)S(1)} %copy-done.7, s32[8,8,256]{2,1,0:T(8,128)S(1)} %copy-done.8, ...), custom_call_target="tpu_custom_call" | custom-call | tf_op jit(solution)/shard_map/first_step/pallas_call | solution.py:299
  58.7 10.6 %all-to-all-start.1 = ((f32[128,1,512]{2,1,0:T(1,128)}), f32[128,1,512]{2,1,0:T(1,128)S(1)}, u32[]{:S(2)}, u32[]{:S(2)}) async-start(f32[128,1,512]{2,1,0:T(1,128)} %bitcast.5), calls=%async_computation.1 | async-start | bytes 524288 | tf_op jit(solution)/shard_map/all_to_all | solution.py:284
  69.3 5.7 %collective-permute-start.7 = (f32[8,1,256]{2,1,0:T(1,128)S(1)}, f32[8,1,256]{2,1,0:T(1,128)S(1)}, u32[]{:S(2)}, u32[]{:S(2)}) collective-permute-start(f32[8,1,256]{2,1,0:T(1,128)S(1)} %get-tuple-element.14), channel_id=1, source_target_pairs={{1,0},{2,1},{3,2},{4,3},{5,4},{6,5},{7,6},{8,7},{9,8},{10,9},{11,1... | collective-permute-start | bytes 24584 | tf_op jit(solution)/shard_map/ppermute | solution.py:278
  74.9 1.9 %collective-permute-start.6 = (f32[8,1,256]{2,1,0:T(1,128)S(1)}, f32[8,1,256]{2,1,0:T(1,128)S(1)}, u32[]{:S(2)}, u32[]{:S(2)}) collective-permute-start(f32[8,1,256]{2,1,0:T(1,128)S(1)} %get-tuple-element.15), channel_id=1, source_target_pairs={{0,1},{1,2},{2,3},{3,4},{4,5},{5,6},{6,7},{7,8},{8,9},{9,10},{10,1... | collective-permute-start | bytes 24584 | tf_op jit(solution)/shard_map/ppermute | solution.py:277
  76.9 2.2 %collective-permute-start.5 = (f32[1,8,256]{2,1,0:T(8,128)S(1)}, f32[1,8,256]{2,1,0:T(8,128)S(1)}, u32[]{:S(2)}, u32[]{:S(2)}) collective-permute-start(f32[1,8,256]{2,1,0:T(8,128)S(1)} %get-tuple-element.16), channel_id=1, source_target_pairs={{16,0},{32,16},{48,32},{64,48},{80,64},{96,80},{112,96},{17,1},{33... | collective-permute-start | bytes 24584 | tf_op jit(solution)/shard_map/ppermute | solution.py:278
  79.1 2.2 %collective-permute-start.4 = (f32[1,8,256]{2,1,0:T(8,128)S(1)}, f32[1,8,256]{2,1,0:T(8,128)S(1)}, u32[]{:S(2)}, u32[]{:S(2)}) collective-permute-start(f32[1,8,256]{2,1,0:T(8,128)S(1)} %get-tuple-element.17), channel_id=1, source_target_pairs={{0,16},{16,32},{32,48},{48,64},{64,80},{80,96},{96,112},{1,17},{17... | collective-permute-start | bytes 24584 | tf_op jit(solution)/shard_map/ppermute | solution.py:277
  81.2 0.0 collective-permute-done.7.right_ref
  81.2 1.4 %collective-permute-done.6.left_ref = f32[8,1,256]{2,1,0:T(1,128)S(1)} collective-permute-done((f32[8,1,256]{2,1,0:T(1,128)S(1)}, f32[8,1,256]{2,1,0:T(1,128)S(1)}, u32[]{:S(2)}, u32[]{:S(2)}) %collective-permute-start.6) | collective-permute-done | bytes 8224 | tf_op jit(solution)/shard_map/ppermute | solution.py:277
  82.6 0.0 collective-permute-done.5.ahead_ref
  82.6 1.4 %collective-permute-done.4.behind_ref = f32[1,8,256]{2,1,0:T(8,128)S(1)} collective-permute-done((f32[1,8,256]{2,1,0:T(8,128)S(1)}, f32[1,8,256]{2,1,0:T(8,128)S(1)}, u32[]{:S(2)}, u32[]{:S(2)}) %collective-permute-start.4) | collective-permute-done | bytes 8224 | tf_op jit(solution)/shard_map/ppermute | solution.py:277
  84.0 0.0 all-to-all-done.1
  84.0 10.6 %second_step.1 = (f32[8,8,256]{2,1,0:T(8,128)}, f32[32,128]{1,0:T(8,128)}) custom-call(f32[512,128]{1,0:T(8,128)S(1)} %bitcast.15, f32[8,8,256]{2,1,0:T(8,128)S(1)} %get-tuple-element.11.air_ref, f32[8,8,256]{2,1,0:T(8,128)S(1)} %copy-done.7, s32[8,8,256]{2,1,0:T(8,128)S(1)} %copy-done.8, f32[32,128]{1,0:T(8,128)S(1)} %get-tuple-element.12.enthalpy_ref, ...), custom_call_target="tpu_custom_call" | custom-call | tf_op jit(solution)/shard_map/second_step/pallas_call | solution.py:307
  (6 shorter events, 0.0 us)
Async XLA Ops:
  0.6 0.7 copy-start.12
  1.3 0.9 copy-start
  2.2 0.9 copy-start.2
  3.1 0.8 copy-start.5
  3.9 0.9 copy-start.9
  4.8 0.7 copy-start.10
  13.3 10.2 %copy-start.6 = (f32[8,8,256]{2,1,0:T(8,128)S(1)}, f32[8,8,256]{2,1,0:T(8,128)}, u32[]{:S(2)}) copy-start(f32[8,8,256]{2,1,0:T(8,128)} %air_ref.3) | copy-start | bytes 196612
  13.3 22.2 %copy-start.1 = (s32[1,128,256]{2,1,0:T(8,128)S(1)}, s32[1,128,256]{2,1,0:T(8,128)}, u32[]{:S(2)}) copy-start(s32[1,128,256]{2,1,0:T(8,128)} %param.14) | copy-start | bytes 393220
  13.3 28.1 %copy-start.11 = (f32[32,128]{1,0:T(8,128)S(1)}, f32[32,128]{1,0:T(8,128)}, u32[]{:S(2)}) copy-start(f32[32,128]{1,0:T(8,128)} %enthalpy_ref.3) | copy-start | bytes 49156
  13.3 28.1 %all-to-all-start = ((f32[128,1,768]{2,1,0:T(1,128)}), f32[128,1,768]{2,1,0:T(1,128)S(1)}, u32[]{:S(2)}, u32[]{:S(2)}) async-start(f32[128,1,768]{2,1,0:T(1,128)} %bitcast.3), calls=%async_computation | async-start | bytes 786432 | tf_op jit(solution)/shard_map/all_to_all | solution.py:284
  23.6 17.8 %copy-start.8 = (s32[8,8,256]{2,1,0:T(8,128)S(1)}, s32[8,8,256]{2,1,0:T(8,128)}, u32[]{:S(2)}) copy-start(s32[8,8,256]{2,1,0:T(8,128)} %fluid_ref.3) | copy-start | bytes 196612
  23.6 17.8 %collective-permute-start.3 = (f32[8,1,256]{2,1,0:T(1,128)S(1)}, f32[8,1,256]{2,1,0:T(1,128)S(1)}, u32[]{:S(2)}, u32[]{:S(2)}) collective-permute-start(f32[8,1,256]{2,1,0:T(1,128)S(1)} %get-tuple-element.18), channel_id=1, source_target_pairs={{1,0},{2,1},{3,2},{4,3},{5,4},{6,5},{7,6},{8,7},{9,8},{10,9},{11,1... | collective-permute-start | bytes 24584 | tf_op jit(solution)/shard_map/ppermute | solution.py:278
  29.3 12.1 %collective-permute-start.2 = (f32[8,1,256]{2,1,0:T(1,128)S(1)}, f32[8,1,256]{2,1,0:T(1,128)S(1)}, u32[]{:S(2)}, u32[]{:S(2)}) collective-permute-start(f32[8,1,256]{2,1,0:T(1,128)S(1)} %get-tuple-element.19), channel_id=1, source_target_pairs={{0,1},{1,2},{2,3},{3,4},{4,5},{5,6},{6,7},{7,8},{8,9},{9,10},{10,1... | collective-permute-start | bytes 24584 | tf_op jit(solution)/shard_map/ppermute | solution.py:277
  31.2 10.2 %collective-permute-start.1 = (f32[1,8,256]{2,1,0:T(8,128)S(1)}, f32[1,8,256]{2,1,0:T(8,128)S(1)}, u32[]{:S(2)}, u32[]{:S(2)}) collective-permute-start(f32[1,8,256]{2,1,0:T(8,128)S(1)} %get-tuple-element.20), channel_id=1, source_target_pairs={{16,0},{32,16},{48,32},{64,48},{80,64},{96,80},{112,96},{17,1},{33... | collective-permute-start | bytes 24584 | tf_op jit(solution)/shard_map/ppermute | solution.py:278
  33.4 8.0 %collective-permute-start = (f32[1,8,256]{2,1,0:T(8,128)S(1)}, f32[1,8,256]{2,1,0:T(8,128)S(1)}, u32[]{:S(2)}, u32[]{:S(2)}) collective-permute-start(f32[1,8,256]{2,1,0:T(8,128)S(1)} %get-tuple-element.21), channel_id=1, source_target_pairs={{0,16},{16,32},{32,48},{48,64},{64,80},{80,96},{96,112},{1,17},{17... | collective-permute-start | bytes 24584 | tf_op jit(solution)/shard_map/ppermute | solution.py:277
  35.6 5.9 %copy-start.3 = (s32[1,128,256]{2,1,0:T(8,128)S(1)}, s32[1,128,256]{2,1,0:T(8,128)}, u32[]{:S(2)}) copy-start(s32[1,128,256]{2,1,0:T(8,128)} %param.17) | copy-start | bytes 393220
  35.6 5.9 %copy-start.4 = (s32[32,8,128]{2,1,0:T(8,128)S(1)}, s32[32,8,128]{2,1,0:T(8,128)}, u32[]{:S(2)}) copy-start(s32[32,8,128]{2,1,0:T(8,128)} %links_ref.3) | copy-start | bytes 393220
  35.6 5.9 %copy-start.7 = (f32[8,8,256]{2,1,0:T(8,128)S(1)}, f32[8,8,256]{2,1,0:T(8,128)}, u32[]{:S(2)}) copy-start(f32[8,8,256]{2,1,0:T(8,128)} %velocity_ref.3) | copy-start | bytes 196612
  58.7 25.4 %all-to-all-start.1 = ((f32[128,1,512]{2,1,0:T(1,128)}), f32[128,1,512]{2,1,0:T(1,128)S(1)}, u32[]{:S(2)}, u32[]{:S(2)}) async-start(f32[128,1,512]{2,1,0:T(1,128)} %bitcast.5), calls=%async_computation.1 | async-start | bytes 524288 | tf_op jit(solution)/shard_map/all_to_all | solution.py:284
  69.3 12.0 %collective-permute-start.7 = (f32[8,1,256]{2,1,0:T(1,128)S(1)}, f32[8,1,256]{2,1,0:T(1,128)S(1)}, u32[]{:S(2)}, u32[]{:S(2)}) collective-permute-start(f32[8,1,256]{2,1,0:T(1,128)S(1)} %get-tuple-element.14), channel_id=1, source_target_pairs={{1,0},{2,1},{3,2},{4,3},{5,4},{6,5},{7,6},{8,7},{9,8},{10,9},{11,1... | collective-permute-start | bytes 24584 | tf_op jit(solution)/shard_map/ppermute | solution.py:278
  74.9 7.7 %collective-permute-start.6 = (f32[8,1,256]{2,1,0:T(1,128)S(1)}, f32[8,1,256]{2,1,0:T(1,128)S(1)}, u32[]{:S(2)}, u32[]{:S(2)}) collective-permute-start(f32[8,1,256]{2,1,0:T(1,128)S(1)} %get-tuple-element.15), channel_id=1, source_target_pairs={{0,1},{1,2},{2,3},{3,4},{4,5},{5,6},{6,7},{7,8},{8,9},{9,10},{10,1... | collective-permute-start | bytes 24584 | tf_op jit(solution)/shard_map/ppermute | solution.py:277
  76.9 5.7 %collective-permute-start.5 = (f32[1,8,256]{2,1,0:T(8,128)S(1)}, f32[1,8,256]{2,1,0:T(8,128)S(1)}, u32[]{:S(2)}, u32[]{:S(2)}) collective-permute-start(f32[1,8,256]{2,1,0:T(8,128)S(1)} %get-tuple-element.16), channel_id=1, source_target_pairs={{16,0},{32,16},{48,32},{64,48},{80,64},{96,80},{112,96},{17,1},{33... | collective-permute-start | bytes 24584 | tf_op jit(solution)/shard_map/ppermute | solution.py:278
  79.1 5.0 %collective-permute-start.4 = (f32[1,8,256]{2,1,0:T(8,128)S(1)}, f32[1,8,256]{2,1,0:T(8,128)S(1)}, u32[]{:S(2)}, u32[]{:S(2)}) collective-permute-start(f32[1,8,256]{2,1,0:T(8,128)S(1)} %get-tuple-element.17), channel_id=1, source_target_pairs={{0,16},{16,32},{32,48},{48,64},{64,80},{80,96},{96,112},{1,17},{17... | collective-permute-start | bytes 24584 | tf_op jit(solution)/shard_map/ppermute | solution.py:277

commit v2 on v1

v2 whole, which is shorter than its diff:
```python
import jax
import jax.numpy as jnp
from jax import lax
from jax.experimental import pallas as pl
from jax.experimental.pallas import tpu as pltpu
from jax.sharding import PartitionSpec as P

LATENT = 1.0
SOLID_SLOPE = 2.0
DT_AIR = 0.1
DT_NODE = 0.05

F32 = jnp.float32
BF16 = jnp.bfloat16
I32 = jnp.int32
LANES = 128
PAIRS = 128
PAIR_ROWS = 256


def node_temp(enthalpy):
    return jnp.where(
        enthalpy < 0.0,
        SOLID_SLOPE * enthalpy,
        jnp.where(enthalpy > LATENT, enthalpy - LATENT, 0.0),
    )


def take(row, lane):
    return jnp.take_along_axis(jnp.broadcast_to(row, lane.shape), lane, axis=1)


def gather(rows, index):
    lane = index & (LANES - 1)
    bits = [((index >> (7 + b)) & 1) == 1 for b in range(len(rows).bit_length() - 1)]

    def pick(first, level):
        if level == 0:
            return take(rows[first], lane)
        low = pick(first, level - 1)
        high = pick(first + (1 << (level - 1)), level - 1)
        return jnp.where(bits[level - 1], high, low)

    return pick(0, len(bits))


def air_rows(air_ref):
    return [
        air_ref[i, j : j + 1, h : h + LANES]
        for i in range(8)
        for j in range(8)
        for h in (0, LANES)
    ]


def iota16():
    return lax.broadcasted_iota(I32, (16, LANES), 0).astype(F32).astype(BF16)


def as_bf16(index):
    return index.astype(F32).astype(BF16)


def two_parts(value):
    top = value.astype(BF16)
    return top, (value - top.astype(F32)).astype(BF16)


def one_hot(index, count, iota):
    one = jnp.ones((16, LANES), BF16)
    zero = jnp.zeros((16, LANES), BF16)
    return jnp.concatenate(
        [jnp.where(index == iota + BF16(16 * i), one, zero) for i in range(count // 16)], axis=0
    )


def weighted(index, values, count, iota):
    zero = jnp.zeros((16, LANES), BF16)
    masks = [index == iota + BF16(16 * i) for i in range(count // 16)]
    return jnp.concatenate(
        [jnp.where(m, part, zero) for v in values for part in two_parts(v) for m in masks], axis=0
    )


def product(rows, high_count, iota):
    left = jnp.concatenate(
        [weighted(as_bf16(high), values, high_count, iota) for high, _, values in rows], axis=1
    )
    right = jnp.concatenate([one_hot(as_bf16(low), LANES, iota) for _, low, _ in rows], axis=1)
    return lax.dot_general(left, right, (((1,), (1,)), ((), ())), preferred_element_type=F32)


def scatter(row_of, high_count, group, beside=None):
    iota = iota16()

    def body(g, acc):
        start = pl.multiple_of(g * group, group)
        acc = acc + product(
            [row_of((start, k), half) for k in range(group) for half in range(2)], high_count, iota
        )
        if beside is not None:
            beside(start)
        return acc

    acc = lax.fori_loop(0, PAIRS // group, body, jnp.zeros((2 * high_count, LANES), F32))
    return acc[:high_count] + acc[high_count:]


def lane_row(ref, row):
    return jnp.broadcast_to(ref[pl.ds(row, 1), :], (16, LANES))


def pair_row(ref, pair, half):
    start, k = pair
    view = ref.at[pl.ds(start, 8 * (k // 8 + 1)), half * LANES : (half + 1) * LANES]
    return jnp.broadcast_to(view[k : k + 1, :], (16, LANES))


def cell_split(cell):
    return ((cell >> 7) & 1) * 64 + (cell >> 8), cell & (LANES - 1)


def node_split(node):
    return node >> 7, node & (LANES - 1)


def to_block(table):
    return jnp.concatenate([table[:64], table[64:]], axis=1).reshape(8, 8, 256)


def every(ref, first, per_pair, start):
    return ref.at[pl.ds(start * per_pair + first, 8, stride=per_pair), :]


def pack_air(air_ref, cell_ref, own_ref, out_ref, per_pair, start, count):
    table = air_rows(air_ref)
    for k in range(0, count, 8):
        at = pl.ds(pl.multiple_of(start + k, 8), 8)
        for half in range(2):
            weight = every(own_ref, 4 + half, 6, start + k)[...]
            values = gather(table, cell_ref[at, half * LANES : (half + 1) * LANES])
            every(out_ref, half, per_pair, start + k)[...] = weight * values


def pack_nodes(warmth_ref, node_ref, out_ref, per_pair, start, count):
    table = [warmth_ref[j : j + 1, :] for j in range(warmth_ref.shape[0])]
    for k in range(0, count, 8):
        at = pl.ds(pl.multiple_of(start + k, 8), 8)
        for half in range(2):
            values = gather(table, node_ref[at, half * LANES : (half + 1) * LANES])
            every(out_ref, 2 + half, per_pair, start + k)[...] = values


def send_out(own_ref, targets, sems, per_pair, start, count):
    at = pl.ds(pl.multiple_of(start * per_pair, 8), count * per_pair)
    for k, target in enumerate(targets):
        pltpu.make_async_copy(own_ref.at[at, :], target.at[at, :], sems.at[k]).start()


def wait_out(own_ref, targets, sems):
    for k, target in enumerate(targets):
        pltpu.make_async_copy(own_ref, target, sems.at[k]).wait()


def pre_kernel(
    air_in, enthalpy_in, cell_in, contact_in, rows_in, node_in, packed_out, kept_out,
    air_ref, enthalpy_ref, cell_ref, contact_ref, rows_ref, node_ref, sems, out_sems,
    warmth_ref, own_ref,
):
    copies = [
        pltpu.make_async_copy(source, target, sems.at[k])
        for k, (source, target) in enumerate(
            [
                (rows_in, rows_ref), (contact_in, contact_ref), (air_in, air_ref),
                (cell_in, cell_ref), (enthalpy_in, enthalpy_ref), (node_in, node_ref),
            ]
        )
    ]
    for copy in copies:
        copy.start()
    for copy in copies:
        copy.wait()
    live = jnp.transpose(jnp.broadcast_to(rows_ref[...], (LANES, LANES)))
    for half in range(2):
        lanes = slice(half * LANES, (half + 1) * LANES)
        spot = lax.broadcasted_iota(I32, (PAIRS, LANES), 1) + half * LANES
        own_ref[pl.ds(4 + half, PAIRS, stride=6), :] = jnp.where(
            spot < live, contact_ref[:, lanes], 0.0
        )
    warmth_ref[...] = node_temp(enthalpy_ref[...])

    def body(g, carry):
        start = pl.multiple_of(g * 32, 32)
        pack_nodes(warmth_ref, node_ref, own_ref, 6, start, 32)
        pack_air(air_ref, cell_ref, own_ref, own_ref, 6, start, 32)
        send_out(own_ref, (packed_out, kept_out), out_sems, 6, start, 32)
        return carry

    lax.fori_loop(0, PAIRS // 32, body, 0)
    wait_out(own_ref, (packed_out, kept_out), out_sems)


def conduction(warmth, links_ref):
    rows = []
    for b in range(warmth.shape[0]):
        linked = take(warmth[b : b + 1], links_ref[b])
        rows.append(jnp.sum(linked, axis=0, keepdims=True))
    return jnp.concatenate(rows, axis=0) - 8.0 * warmth


def air_step(air, velocity, fluid, behind_halo, ahead_halo, left_halo, right_halo, source):
    behind = jnp.concatenate([behind_halo, air[:-1]], axis=0)
    ahead = jnp.concatenate([air[1:], ahead_halo], axis=0)
    row = lax.broadcasted_iota(I32, air.shape, 1)
    lane = lax.broadcasted_iota(I32, air.shape, 2)
    low = jnp.where(row == 0, left_halo, pltpu.roll(air, 1, 1))
    high = jnp.where(row == 7, right_halo, pltpu.roll(air, 7, 1))
    flat = air.reshape(64, 256)
    left = jnp.where(lane == 0, 0.0, pltpu.roll(flat, 1, 1).reshape(air.shape))
    right = jnp.where(lane == 255, 0.0, pltpu.roll(flat, 255, 1).reshape(air.shape))
    laplace = (ahead + behind) + (high + low) + (right + left) - 6.0 * air
    advect = jnp.maximum(velocity, 0.0) * (air - behind) + jnp.minimum(velocity, 0.0) * (
        ahead - air
    )
    return air + fluid.astype(F32) * DT_AIR * (laplace - advect + source)


def air_part(
    own_ref, received_ref, first_ref, per_pair, air_ref, velocity_ref, fluid_ref, cell_ref,
    edge_refs, air_out_ref, beside,
):
    def heat_row(pair, half):
        p = pair[0] + pair[1]
        base = p * per_pair + half
        heat = lane_row(first_ref, p * 6 + 4 + half) * lane_row(received_ref, base + 2)
        heat = heat - lane_row(own_ref, base)
        return cell_split(pair_row(cell_ref, pair, half)) + ([heat],)

    heat = scatter(heat_row, 128, 32, beside)
    edges = []
    for axis, refs in (("len", edge_refs[:2]), ("hgt", edge_refs[2:])):
        at = lax.axis_index(axis)
        for ref, last in zip(refs, (0, lax.axis_size(axis) - 1)):
            edges.append(jnp.where(at == last, 0.0, ref[...]))
    air_out_ref[...] = air_step(
        air_ref[...], velocity_ref[...], fluid_ref[...], *edges, to_block(heat)
    )


def node_part(own_ref, received_ref, first_ref, per_pair, enthalpy_ref, links_ref, node_ref):
    def node_row(pair, half):
        p = pair[0] + pair[1]
        base = p * per_pair + half
        heat = lane_row(first_ref, p * 6 + 4 + half) * lane_row(own_ref, base + 2)
        heat = lane_row(received_ref, base) - heat
        return node_split(pair_row(node_ref, pair, half)) + ([heat],)

    gained = scatter(node_row, 32, 32)
    enthalpy = enthalpy_ref[...]
    return enthalpy + DT_NODE * (conduction(node_temp(enthalpy), links_ref) + gained)


def mid_kernel(
    own_ref, first_ref, air_ref, velocity_ref, fluid_ref, enthalpy_ref, links_ref, cell_ref,
    node_ref, behind_ref, ahead_ref, left_ref, right_ref,
    air_out_ref, enthalpy_out_ref, next_ref, packed_out, warmth_ref, out_sems,
):
    enthalpy = node_part(own_ref, first_ref, first_ref, 6, enthalpy_ref, links_ref, node_ref)
    enthalpy_out_ref[...] = enthalpy
    warmth_ref[...] = node_temp(enthalpy)
    air_part(
        own_ref, first_ref, own_ref, 6, air_ref, velocity_ref, fluid_ref, cell_ref,
        (behind_ref, ahead_ref, left_ref, right_ref), air_out_ref,
        lambda start: pack_nodes(warmth_ref, node_ref, next_ref, 4, start, 32),
    )

    def body(g, carry):
        start = pl.multiple_of(g * 32, 32)
        pack_air(air_out_ref, cell_ref, own_ref, next_ref, 4, start, 32)
        send_out(next_ref, (packed_out,), out_sems, 4, start, 32)
        return carry

    lax.fori_loop(0, PAIRS // 32, body, 0)
    wait_out(next_ref, (packed_out,), out_sems)


def post_kernel(
    kept_ref, own_ref, received_ref, first_ref, air_ref, velocity_ref, fluid_ref, enthalpy_ref,
    links_ref, cell_ref, node_ref, behind_ref, ahead_ref, left_ref, right_ref,
    air_out_ref, enthalpy_out_ref,
):
    enthalpy_out_ref[...] = node_part(
        own_ref, received_ref, first_ref, 4, enthalpy_ref, links_ref, node_ref
    )
    air_part(
        own_ref, received_ref, kept_ref, 4, air_ref, velocity_ref, fluid_ref, cell_ref,
        (behind_ref, ahead_ref, left_ref, right_ref), air_out_ref, None,
    )


VMEM = pl.BlockSpec(memory_space=pltpu.VMEM)
HBM = pl.BlockSpec(memory_space=pltpu.HBM)


def call(kernel, name, shapes, mebibytes, **options):
    return pl.pallas_call(
        kernel,
        out_shape=[jax.ShapeDtypeStruct(s, F32) for s in shapes],
        name=name,
        compiler_params=pltpu.CompilerParams(vmem_limit_bytes=mebibytes * 1024 * 1024),
        **options,
    )


def halos(air):
    out = []
    for axis, dim in (("len", 0), ("hgt", 1)):
        count = lax.axis_size(axis)
        ring = [(i, (i + 1) % count) for i in range(count)]
        head = lax.slice_in_dim(air, 0, 1, axis=dim)
        tail = lax.slice_in_dim(air, air.shape[dim] - 1, air.shape[dim], axis=dim)
        out.append(lax.ppermute(tail, axis, ring))
        out.append(lax.ppermute(head, axis, [(j, i) for i, j in ring]))
    return out


def exchange(packed):
    both = packed.reshape(PAIRS, 1, -1)
    both = lax.all_to_all(both, ("len", "hgt"), split_axis=0, concat_axis=0, tiled=True)
    return both.reshape(packed.shape)


def local(
    air_temp, velocity, fluid, enthalpy, adjacency_lists, send_cells, contact, pair_rows, recv_nodes
):
    cells, nodes = send_cells[0], recv_nodes[0]
    block, panel = air_temp.shape, enthalpy.shape
    arrays = (air_temp, enthalpy, cells, contact[0], pair_rows, nodes)
    wide, narrow = (6 * PAIRS, LANES), (4 * PAIRS, LANES)
    packed, kept = call(
        pre_kernel,
        "pack_first",
        [wide, wide],
        60,
        in_specs=[HBM] * len(arrays),
        out_specs=[HBM, HBM],
        scratch_shapes=[pltpu.VMEM(x.shape, x.dtype) for x in arrays]
        + [pltpu.SemaphoreType.DMA((len(arrays),)), pltpu.SemaphoreType.DMA((2,))]
        + [pltpu.VMEM(panel, F32), pltpu.VMEM(wide, F32)],
    )(*arrays)
    first = exchange(packed)
    edges = halos(air_temp)
    air, heat, own, packed = call(
        mid_kernel,
        "first_step",
        [block, panel, narrow, narrow],
        32,
        out_specs=[VMEM, VMEM, VMEM, HBM],
        scratch_shapes=[pltpu.VMEM(panel, F32), pltpu.SemaphoreType.DMA((1,))],
    )(
        kept, first, air_temp, velocity, fluid, enthalpy, adjacency_lists, cells, nodes, *edges
    )
    received = exchange(packed)
    edges = halos(air)
    air, heat = call(post_kernel, "second_step", [block, panel], 32)(
        kept, own, received, first, air, velocity, fluid, heat, adjacency_lists, cells, nodes,
        *edges,
    )
    return air, heat


def solution(mesh):
    rows = P(("len", "hgt"), None)
    lists = P(("len", "hgt"), None, None)
    grid = P("len", "hgt", None)
    in_specs = (grid, grid, grid, rows, lists, lists, lists, rows, lists)
    return jax.shard_map(
        local, mesh=mesh, in_specs=in_specs, out_specs=(grid, rows), check_vma=False
    )
```

time: 95.2 us -> 74.5 us (0.78)
  the two profiles are of different devices: /device:TPU:30 before, /device:TPU:1 now
where the time goes in v2:
time: 74.5 us; the launch traced here: 74.1 us
  starting transfers between devices  32.7 us (44%)
  Pallas kernels  31.5 us (42%)
  waiting for transfers between devices  9.05 us (12%)
  between operations  0.8 us (1%)
    all_to_all x2, starting transfers between devices, exchange(): lax.all_to_all(both, ('len', 'hgt'), split_axis=0, concat_axis=0, tiled=T...  18.1 us
    pallas_call x1, Pallas kernels, local(): call(mid_kernel, 'first_step', [block, panel, narrow, narrow], 32, out_sp...  14.2 us
    ppermute x4, starting transfers between devices, halos(): out.append(lax.ppermute(head, axis, [(j, i) for i, j in ring]))  12.3 us
    pallas_call x1, Pallas kernels, local(): call(post_kernel, 'second_step', [block, panel], 32)  9.45 us
    ppermute x4, waiting for transfers between devices, halos(): out.append(lax.ppermute(tail, axis, ring))  8.57 us
    pallas_call x1, Pallas kernels, local(): call(pre_kernel, 'pack_first', [wide, wide], 60, in_specs=[HBM] * len(arr...  7.89 us
    ppermute x4, starting transfers between devices, halos(): out.append(lax.ppermute(tail, axis, ring))  2.31 us
  transfers between devices with their start and end apart: 10, of which 3 were waited for; matrix products, arithmetic and copies ran while one was open for 0% of the time, Pallas kernels for 0%

profile of v2, /device:TPU:1, one launch (start us, length us, event | category | flops | bytes accessed | tf_op | source)
XLA Modules:
  0.0 74.1 jit_solution(2570505611533388846)
XLA Ops:
  0.6 0.0 copy-start.4
  0.6 0.0 copy-start.6
  0.7 0.0 copy-start.7
  0.7 7.9 %pack_first.1 = (f32[768,128]{1,0:T(8,128)}, f32[768,128]{1,0:T(8,128)}) custom-call(f32[8,8,256]{2,1,0:T(8,128)} %air_ref.1, f32[32,128]{1,0:T(8,128)} %enthalpy_ref.1, s32[128,256]{1,0:T(8,128)} %bitcast.9, f32[128,256]{1,0:T(8,128)} %bitcast.17, s32[1,128]{1,0:T(1,128)} %rows_in.1, s32[128,256]{1,0:T(8,128)} %bitcast.12), custom_call_target="tpu_custom_call" | custom-call | tf_op jit(solution)/shard_map/pack_first/pallas_call | solution.py:340
  8.6 0.0 copy-start
  8.6 0.0 copy-start.1
  8.6 0.0 copy-start.2
  8.6 0.0 copy-start.3
  8.6 11.5 %all-to-all-start = ((f32[128,1,768]{2,1,0:T(1,128)}), f32[128,1,768]{2,1,0:T(1,128)S(1)}, u32[]{:S(2)}, u32[]{:S(2)}) async-start(f32[128,1,768]{2,1,0:T(1,128)} %bitcast.16), calls=%async_computation | async-start | bytes 786432 | tf_op jit(solution)/shard_map/all_to_all | solution.py:329
  20.1 0.0 copy-done.4
  20.1 0.0 copy-start.5
  20.2 5.5 %collective-permute-start.3 = (f32[8,1,256]{2,1,0:T(1,128)S(1)}, f32[8,1,256]{2,1,0:T(1,128)S(1)}, u32[]{:S(2)}, u32[]{:S(2)}) collective-permute-start(f32[8,1,256]{2,1,0:T(1,128)S(1)} %get-tuple-element.18), channel_id=1, source_target_pairs={{1,0},{2,1},{3,2},{4,3},{5,4},{6,5},{7,6},{8,7},{9,8},{10,9},{11,1... | collective-permute-start | bytes 24584 | tf_op jit(solution)/shard_map/ppermute | solution.py:323
  25.6 0.0 collective-permute-start.2
  25.6 0.6 collective-permute-start.1
  26.3 1.2 %collective-permute-start = (f32[1,8,256]{2,1,0:T(8,128)S(1)}, f32[1,8,256]{2,1,0:T(8,128)S(1)}, u32[]{:S(2)}, u32[]{:S(2)}) collective-permute-start(f32[1,8,256]{2,1,0:T(8,128)S(1)} %get-tuple-element.21), channel_id=1, source_target_pairs={{0,16},{16,32},{32,48},{48,64},{64,80},{80,96},{96,112},{112,0},{1... | collective-permute-start | bytes 24584 | tf_op jit(solution)/shard_map/ppermute | solution.py:322
  27.4 0.0 collective-permute-done.3.right_ref
  27.4 4.3 %collective-permute-done.2.left_ref = f32[8,1,256]{2,1,0:T(1,128)S(1)} collective-permute-done((f32[8,1,256]{2,1,0:T(1,128)S(1)}, f32[8,1,256]{2,1,0:T(1,128)S(1)}, u32[]{:S(2)}, u32[]{:S(2)}) %collective-permute-start.2) | collective-permute-done | bytes 8224 | tf_op jit(solution)/shard_map/ppermute | solution.py:322
  31.8 0.0 collective-permute-done.1.ahead_ref
  31.8 0.0 collective-permute-done.behind_ref
  31.8 0.5 all-to-all-done
  32.2 0.0 copy-done.6
  32.2 0.0 copy-done.7
  32.2 0.0 copy-done
  32.2 0.0 copy-done.1
  32.3 0.0 copy-done.2
  32.3 0.0 copy-done.3
  32.3 0.0 copy-done.5
  32.3 14.2 %first_step.1 = (f32[8,8,256]{2,1,0:T(8,128)S(1)}, f32[32,128]{1,0:T(8,128)S(1)}, f32[512,128]{1,0:T(8,128)S(1)}, f32[512,128]{1,0:T(8,128)}) custom-call(f32[768,128]{1,0:T(8,128)S(1)} %copy-done, f32[768,128]{1,0:T(8,128)S(1)} %bitcast.7, f32[8,8,256]{2,1,0:T(8,128)S(1)} %copy-done.4, f32[8,8,256]{2,1,0:T(8,128)S(1)} %copy-done.5, ...), custom_call_target="tpu_custom_call" | custom-call | tf_op jit(solution)/shard_map/first_step/pallas_call | solution.py:353
  46.5 6.6 %all-to-all-start.1 = ((f32[128,1,512]{2,1,0:T(1,128)}), f32[128,1,512]{2,1,0:T(1,128)S(1)}, u32[]{:S(2)}, u32[]{:S(2)}) async-start(f32[128,1,512]{2,1,0:T(1,128)} %bitcast.5), calls=%async_computation.1 | async-start | bytes 524288 | tf_op jit(solution)/shard_map/all_to_all | solution.py:329
  53.1 5.5 %collective-permute-start.7 = (f32[8,1,256]{2,1,0:T(1,128)S(1)}, f32[8,1,256]{2,1,0:T(1,128)S(1)}, u32[]{:S(2)}, u32[]{:S(2)}) collective-permute-start(f32[8,1,256]{2,1,0:T(1,128)S(1)} %get-tuple-element.14), channel_id=1, source_target_pairs={{1,0},{2,1},{3,2},{4,3},{5,4},{6,5},{7,6},{8,7},{9,8},{10,9},{11,1... | collective-permute-start | bytes 24584 | tf_op jit(solution)/shard_map/ppermute | solution.py:323
  58.6 0.0 collective-permute-start.6
  58.6 0.6 collective-permute-start.5
  59.2 1.2 %collective-permute-start.4 = (f32[1,8,256]{2,1,0:T(8,128)S(1)}, f32[1,8,256]{2,1,0:T(8,128)S(1)}, u32[]{:S(2)}, u32[]{:S(2)}) collective-permute-start(f32[1,8,256]{2,1,0:T(8,128)S(1)} %get-tuple-element.17), channel_id=1, source_target_pairs={{0,16},{16,32},{32,48},{48,64},{64,80},{80,96},{96,112},{112,0},{1... | collective-permute-start | bytes 24584 | tf_op jit(solution)/shard_map/ppermute | solution.py:322
  60.4 0.0 collective-permute-done.7.right_ref
  60.4 4.2 %collective-permute-done.6.left_ref = f32[8,1,256]{2,1,0:T(1,128)S(1)} collective-permute-done((f32[8,1,256]{2,1,0:T(1,128)S(1)}, f32[8,1,256]{2,1,0:T(1,128)S(1)}, u32[]{:S(2)}, u32[]{:S(2)}) %collective-permute-start.6) | collective-permute-done | bytes 8224 | tf_op jit(solution)/shard_map/ppermute | solution.py:322
  64.6 0.0 collective-permute-done.5.ahead_ref
  64.6 0.0 collective-permute-done.4.behind_ref
  64.7 0.0 all-to-all-done.1
  64.7 9.4 %second_step.1 = (f32[8,8,256]{2,1,0:T(8,128)}, f32[32,128]{1,0:T(8,128)}) custom-call(f32[768,128]{1,0:T(8,128)S(1)} %copy-done, f32[512,128]{1,0:T(8,128)S(1)} %get-tuple-element.10.own_ref, f32[512,128]{1,0:T(8,128)S(1)} %bitcast.15, f32[768,128]{1,0:T(8,128)S(1)} %bitcast.8, f32[8,8,256]{2,1,0:T(8,128)S(1)} %get-tuple-element.12.air_ref, ...), custom_call_target="tpu_custom_call" | custom-call | tf_op jit(solution)/shard_map/second_step/pallas_call | solution.py:365
  (4 shorter events, 0.0 us)
Async XLA Ops:
  0.6 19.5 %copy-start.4 = (f32[8,8,256]{2,1,0:T(8,128)S(1)}, f32[8,8,256]{2,1,0:T(8,128)}, u32[]{:S(2)}) copy-start(f32[8,8,256]{2,1,0:T(8,128)} %air_ref.1) | copy-start | bytes 196612
  0.6 31.6 %copy-start.6 = (s32[8,8,256]{2,1,0:T(8,128)S(1)}, s32[8,8,256]{2,1,0:T(8,128)}, u32[]{:S(2)}) copy-start(s32[8,8,256]{2,1,0:T(8,128)} %fluid_ref.3) | copy-start | bytes 196612
  0.7 31.6 %copy-start.7 = (f32[32,128]{1,0:T(8,128)S(1)}, f32[32,128]{1,0:T(8,128)}, u32[]{:S(2)}) copy-start(f32[32,128]{1,0:T(8,128)} %enthalpy_ref.1) | copy-start | bytes 49156
  8.6 23.7 %copy-start = (f32[768,128]{1,0:T(8,128)S(1)}, f32[768,128]{1,0:T(8,128)}, u32[]{:S(2)}) copy-start(f32[768,128]{1,0:T(8,128)} %get-tuple-element.8.own_ref.kept_ref) | copy-start | bytes 1179652
  8.6 23.7 %copy-start.1 = (s32[1,128,256]{2,1,0:T(8,128)S(1)}, s32[1,128,256]{2,1,0:T(8,128)}, u32[]{:S(2)}) copy-start(s32[1,128,256]{2,1,0:T(8,128)} %param.14) | copy-start | bytes 393220
  8.6 23.7 %copy-start.2 = (s32[1,128,256]{2,1,0:T(8,128)S(1)}, s32[1,128,256]{2,1,0:T(8,128)}, u32[]{:S(2)}) copy-start(s32[1,128,256]{2,1,0:T(8,128)} %param.17) | copy-start | bytes 393220
  8.6 23.7 %copy-start.3 = (s32[32,8,128]{2,1,0:T(8,128)S(1)}, s32[32,8,128]{2,1,0:T(8,128)}, u32[]{:S(2)}) copy-start(s32[32,8,128]{2,1,0:T(8,128)} %links_ref.3) | copy-start | bytes 393220
  8.6 23.6 %all-to-all-start = ((f32[128,1,768]{2,1,0:T(1,128)}), f32[128,1,768]{2,1,0:T(1,128)S(1)}, u32[]{:S(2)}, u32[]{:S(2)}) async-start(f32[128,1,768]{2,1,0:T(1,128)} %bitcast.16), calls=%async_computation | async-start | bytes 786432 | tf_op jit(solution)/shard_map/all_to_all | solution.py:329
  20.1 12.2 %copy-start.5 = (f32[8,8,256]{2,1,0:T(8,128)S(1)}, f32[8,8,256]{2,1,0:T(8,128)}, u32[]{:S(2)}) copy-start(f32[8,8,256]{2,1,0:T(8,128)} %velocity_ref.3) | copy-start | bytes 196612
  20.2 7.3 %collective-permute-start.3 = (f32[8,1,256]{2,1,0:T(1,128)S(1)}, f32[8,1,256]{2,1,0:T(1,128)S(1)}, u32[]{:S(2)}, u32[]{:S(2)}) collective-permute-start(f32[8,1,256]{2,1,0:T(1,128)S(1)} %get-tuple-element.18), channel_id=1, source_target_pairs={{1,0},{2,1},{3,2},{4,3},{5,4},{6,5},{7,6},{8,7},{9,8},{10,9},{11,1... | collective-permute-start | bytes 24584 | tf_op jit(solution)/shard_map/ppermute | solution.py:323
  25.6 6.1 %collective-permute-start.2 = (f32[8,1,256]{2,1,0:T(1,128)S(1)}, f32[8,1,256]{2,1,0:T(1,128)S(1)}, u32[]{:S(2)}, u32[]{:S(2)}) collective-permute-start(f32[8,1,256]{2,1,0:T(1,128)S(1)} %get-tuple-element.19), channel_id=1, source_target_pairs={{0,1},{1,2},{2,3},{3,4},{4,5},{5,6},{6,7},{7,8},{8,9},{9,10},{10,1... | collective-permute-start | bytes 24584 | tf_op jit(solution)/shard_map/ppermute | solution.py:322
  25.6 6.1 %collective-permute-start.1 = (f32[1,8,256]{2,1,0:T(8,128)S(1)}, f32[1,8,256]{2,1,0:T(8,128)S(1)}, u32[]{:S(2)}, u32[]{:S(2)}) collective-permute-start(f32[1,8,256]{2,1,0:T(8,128)S(1)} %get-tuple-element.20), channel_id=1, source_target_pairs={{16,0},{32,16},{48,32},{64,48},{80,64},{96,80},{112,96},{0,112},{1... | collective-permute-start | bytes 24584 | tf_op jit(solution)/shard_map/ppermute | solution.py:323
  26.3 5.5 %collective-permute-start = (f32[1,8,256]{2,1,0:T(8,128)S(1)}, f32[1,8,256]{2,1,0:T(8,128)S(1)}, u32[]{:S(2)}, u32[]{:S(2)}) collective-permute-start(f32[1,8,256]{2,1,0:T(8,128)S(1)} %get-tuple-element.21), channel_id=1, source_target_pairs={{0,16},{16,32},{32,48},{48,64},{64,80},{80,96},{96,112},{112,0},{1... | collective-permute-start | bytes 24584 | tf_op jit(solution)/shard_map/ppermute | solution.py:322
  46.5 18.2 %all-to-all-start.1 = ((f32[128,1,512]{2,1,0:T(1,128)}), f32[128,1,512]{2,1,0:T(1,128)S(1)}, u32[]{:S(2)}, u32[]{:S(2)}) async-start(f32[128,1,512]{2,1,0:T(1,128)} %bitcast.5), calls=%async_computation.1 | async-start | bytes 524288 | tf_op jit(solution)/shard_map/all_to_all | solution.py:329
  53.1 7.3 %collective-permute-start.7 = (f32[8,1,256]{2,1,0:T(1,128)S(1)}, f32[8,1,256]{2,1,0:T(1,128)S(1)}, u32[]{:S(2)}, u32[]{:S(2)}) collective-permute-start(f32[8,1,256]{2,1,0:T(1,128)S(1)} %get-tuple-element.14), channel_id=1, source_target_pairs={{1,0},{2,1},{3,2},{4,3},{5,4},{6,5},{7,6},{8,7},{9,8},{10,9},{11,1... | collective-permute-start | bytes 24584 | tf_op jit(solution)/shard_map/ppermute | solution.py:323
  58.6 6.1 %collective-permute-start.6 = (f32[8,1,256]{2,1,0:T(1,128)S(1)}, f32[8,1,256]{2,1,0:T(1,128)S(1)}, u32[]{:S(2)}, u32[]{:S(2)}) collective-permute-start(f32[8,1,256]{2,1,0:T(1,128)S(1)} %get-tuple-element.15), channel_id=1, source_target_pairs={{0,1},{1,2},{2,3},{3,4},{4,5},{5,6},{6,7},{7,8},{8,9},{9,10},{10,1... | collective-permute-start | bytes 24584 | tf_op jit(solution)/shard_map/ppermute | solution.py:322
  58.6 6.0 %collective-permute-start.5 = (f32[1,8,256]{2,1,0:T(8,128)S(1)}, f32[1,8,256]{2,1,0:T(8,128)S(1)}, u32[]{:S(2)}, u32[]{:S(2)}) collective-permute-start(f32[1,8,256]{2,1,0:T(8,128)S(1)} %get-tuple-element.16), channel_id=1, source_target_pairs={{16,0},{32,16},{48,32},{64,48},{80,64},{96,80},{112,96},{0,112},{1... | collective-permute-start | bytes 24584 | tf_op jit(solution)/shard_map/ppermute | solution.py:323
  59.2 5.4 %collective-permute-start.4 = (f32[1,8,256]{2,1,0:T(8,128)S(1)}, f32[1,8,256]{2,1,0:T(8,128)S(1)}, u32[]{:S(2)}, u32[]{:S(2)}) collective-permute-start(f32[1,8,256]{2,1,0:T(8,128)S(1)} %get-tuple-element.17), channel_id=1, source_target_pairs={{0,16},{16,32},{32,48},{48,64},{64,80},{80,96},{96,112},{112,0},{1... | collective-permute-start | bytes 24584 | tf_op jit(solution)/shard_map/ppermute | solution.py:322

commit v3 on v2

--- a/solution.py
+++ b/solution.py
@@ -132,23 +132,62 @@
     return ref.at[pl.ds(start * per_pair + first, 8, stride=per_pair), :]
 
 
-def pack_air(air_ref, cell_ref, own_ref, out_ref, per_pair, start, count):
+def turned(air_ref):
+    flat = air_ref[...].reshape(64, 256)
+    table = jnp.transpose(jnp.concatenate([flat[:, :LANES], flat[:, LANES:]], axis=0))
+    return jnp.concatenate(two_parts(table), axis=1)
+
+
+def gather_by_product(table, cells):
+    iota = iota16()
+    count = lax.broadcasted_iota(I32, (8, LANES), 0)
+    hots, lows = [], []
+    for cell in cells:
+        for k in range(8):
+            high, low = cell_split(jnp.broadcast_to(cell[k : k + 1], (16, LANES)))
+            hots.append(one_hot(as_bf16(high), LANES, iota))
+            lows.append(low[:8])
+    hots = jnp.concatenate(hots, axis=1)
+    found = lax.dot_general(
+        table,
+        jnp.concatenate([hots, hots], axis=0),
+        (((1,), (0,)), ((), ())),
+        preferred_element_type=F32,
+    )
+    rows = []
+    for n, low in enumerate(lows):
+        column = found[:, n * LANES : (n + 1) * LANES]
+        level = [column[k : k + 8] for k in range(0, LANES, 8)]
+        for b in range(3, 7):
+            bit = ((low >> b) & 1) == 1
+            level = [jnp.where(bit, y, x) for x, y in zip(level[::2], level[1::2])]
+        rows.append(
+            jnp.sum(jnp.where((low & 7) == count, level[0], 0.0), axis=0, keepdims=True)
+        )
+    return [jnp.concatenate(rows[k : k + 8], axis=0) for k in range(0, len(rows), 8)]
+
+
+def pack_air(air_ref, turned_ref, cell_ref, own_ref, out_ref, per_pair, start, count, by_lane):
     table = air_rows(air_ref)
-    for k in range(0, count, 8):
-        at = pl.ds(pl.multiple_of(start + k, 8), 8)
-        for half in range(2):
-            weight = every(own_ref, 4 + half, 6, start + k)[...]
-            values = gather(table, cell_ref[at, half * LANES : (half + 1) * LANES])
-            every(out_ref, half, per_pair, start + k)[...] = weight * values
-
-
-def pack_nodes(warmth_ref, node_ref, out_ref, per_pair, start, count):
+    blocks = [(k, half) for k in range(0, count, 8) for half in range(2)]
+    cells = [
+        cell_ref[pl.ds(pl.multiple_of(start + k, 8), 8), half * LANES : (half + 1) * LANES]
+        for k, half in blocks
+    ]
+    found = gather_by_product(turned_ref[...], cells[by_lane:])
+    found = [gather(table, cell) for cell in cells[:by_lane]] + found
+    for (k, half), values in zip(blocks, found):
+        weight = every(own_ref, 4 + half, 6, start + k)[...]
+        every(out_ref, half, per_pair, start + k)[...] = weight * values
+
+
+def pack_nodes(warmth_ref, node_ref, out_ref, per_pair, first, start, count):
     table = [warmth_ref[j : j + 1, :] for j in range(warmth_ref.shape[0])]
     for k in range(0, count, 8):
         at = pl.ds(pl.multiple_of(start + k, 8), 8)
         for half in range(2):
             values = gather(table, node_ref[at, half * LANES : (half + 1) * LANES])
-            every(out_ref, 2 + half, per_pair, start + k)[...] = values
+            every(out_ref, first + half, per_pair, start + k)[...] = values
 
 
 def send_out(own_ref, targets, sems, per_pair, start, count):
@@ -165,7 +204,7 @@
 def pre_kernel(
     air_in, enthalpy_in, cell_in, contact_in, rows_in, node_in, packed_out, kept_out,
     air_ref, enthalpy_ref, cell_ref, contact_ref, rows_ref, node_ref, sems, out_sems,
-    warmth_ref, own_ref,
+    warmth_ref, turned_ref, own_ref,
 ):
     copies = [
         pltpu.make_async_copy(source, target, sems.at[k])
@@ -188,11 +227,12 @@
             spot < live, contact_ref[:, lanes], 0.0
         )
     warmth_ref[...] = node_temp(enthalpy_ref[...])
+    turned_ref[...] = turned(air_ref)
 
     def body(g, carry):
         start = pl.multiple_of(g * 32, 32)
-        pack_nodes(warmth_ref, node_ref, own_ref, 6, start, 32)
-        pack_air(air_ref, cell_ref, own_ref, own_ref, 6, start, 32)
+        pack_nodes(warmth_ref, node_ref, own_ref, 6, 2, start, 32)
+        pack_air(air_ref, turned_ref, cell_ref, own_ref, own_ref, 6, start, 32, 2)
         send_out(own_ref, (packed_out, kept_out), out_sems, 6, start, 32)
         return carry
 
@@ -225,10 +265,7 @@
     return air + fluid.astype(F32) * DT_AIR * (laplace - advect + source)
 
 
-def air_part(
-    own_ref, received_ref, first_ref, per_pair, air_ref, velocity_ref, fluid_ref, cell_ref,
-    edge_refs, air_out_ref, beside,
-):
+def heat_part(own_ref, received_ref, first_ref, per_pair, cell_ref, heat_ref, beside=None):
     def heat_row(pair, half):
         p = pair[0] + pair[1]
         base = p * per_pair + half
@@ -236,14 +273,17 @@
         heat = heat - lane_row(own_ref, base)
         return cell_split(pair_row(cell_ref, pair, half)) + ([heat],)
 
-    heat = scatter(heat_row, 128, 32, beside)
+    heat_ref[...] = to_block(scatter(heat_row, 128, 32, beside))
+
+
+def air_part(heat_ref, air_ref, velocity_ref, fluid_ref, edge_refs, air_out_ref):
     edges = []
     for axis, refs in (("len", edge_refs[:2]), ("hgt", edge_refs[2:])):
         at = lax.axis_index(axis)
         for ref, last in zip(refs, (0, lax.axis_size(axis) - 1)):
             edges.append(jnp.where(at == last, 0.0, ref[...]))
     air_out_ref[...] = air_step(
-        air_ref[...], velocity_ref[...], fluid_ref[...], *edges, to_block(heat)
+        air_ref[...], velocity_ref[...], fluid_ref[...], *edges, heat_ref[...]
     )
 
 
@@ -260,23 +300,34 @@
     return enthalpy + DT_NODE * (conduction(node_temp(enthalpy), links_ref) + gained)
 
 
-def mid_kernel(
-    own_ref, first_ref, air_ref, velocity_ref, fluid_ref, enthalpy_ref, links_ref, cell_ref,
-    node_ref, behind_ref, ahead_ref, left_ref, right_ref,
-    air_out_ref, enthalpy_out_ref, next_ref, packed_out, warmth_ref, out_sems,
+def mid_sums_kernel(
+    own_ref, first_ref, enthalpy_ref, links_ref, cell_ref, node_ref,
+    enthalpy_out_ref, heat_ref, surface_ref, warmth_ref,
 ):
     enthalpy = node_part(own_ref, first_ref, first_ref, 6, enthalpy_ref, links_ref, node_ref)
     enthalpy_out_ref[...] = enthalpy
     warmth_ref[...] = node_temp(enthalpy)
+    heat_part(
+        own_ref, first_ref, own_ref, 6, cell_ref, heat_ref,
+        lambda start: pack_nodes(warmth_ref, node_ref, surface_ref, 2, 0, start, 32),
+    )
+
+
+def mid_air_kernel(
+    own_ref, heat_ref, surface_ref, air_ref, velocity_ref, fluid_ref, cell_ref, behind_ref,
+    ahead_ref, left_ref, right_ref, air_out_ref, next_ref, packed_out, turned_ref, out_sems,
+):
     air_part(
-        own_ref, first_ref, own_ref, 6, air_ref, velocity_ref, fluid_ref, cell_ref,
-        (behind_ref, ahead_ref, left_ref, right_ref), air_out_ref,
-        lambda start: pack_nodes(warmth_ref, node_ref, next_ref, 4, start, 32),
-    )
+        heat_ref, air_ref, velocity_ref, fluid_ref, (behind_ref, ahead_ref, left_ref, right_ref),
+        air_out_ref,
+    )
+    turned_ref[...] = turned(air_out_ref)
+    for half in range(2):
+        next_ref[pl.ds(2 + half, PAIRS, stride=4), :] = surface_ref[pl.ds(half, PAIRS, stride=2), :]
 
     def body(g, carry):
         start = pl.multiple_of(g * 32, 32)
-        pack_air(air_out_ref, cell_ref, own_ref, next_ref, 4, start, 32)
+        pack_air(air_out_ref, turned_ref, cell_ref, own_ref, next_ref, 4, start, 32, 3)
         send_out(next_ref, (packed_out,), out_sems, 4, start, 32)
         return carry
 
@@ -284,17 +335,23 @@
     wait_out(next_ref, (packed_out,), out_sems)
 
 
-def post_kernel(
-    kept_ref, own_ref, received_ref, first_ref, air_ref, velocity_ref, fluid_ref, enthalpy_ref,
-    links_ref, cell_ref, node_ref, behind_ref, ahead_ref, left_ref, right_ref,
-    air_out_ref, enthalpy_out_ref,
+def post_sums_kernel(
+    kept_ref, own_ref, received_ref, first_ref, enthalpy_ref, links_ref, cell_ref, node_ref,
+    enthalpy_out_ref, heat_ref,
 ):
     enthalpy_out_ref[...] = node_part(
         own_ref, received_ref, first_ref, 4, enthalpy_ref, links_ref, node_ref
     )
+    heat_part(own_ref, received_ref, kept_ref, 4, cell_ref, heat_ref)
+
+
+def post_air_kernel(
+    heat_ref, air_ref, velocity_ref, fluid_ref, behind_ref, ahead_ref, left_ref, right_ref,
+    air_out_ref,
+):
     air_part(
-        own_ref, received_ref, kept_ref, 4, air_ref, velocity_ref, fluid_ref, cell_ref,
-        (behind_ref, ahead_ref, left_ref, right_ref), air_out_ref, None,
+        heat_ref, air_ref, velocity_ref, fluid_ref, (behind_ref, ahead_ref, left_ref, right_ref),
+        air_out_ref,
     )
 
 
@@ -346,27 +403,35 @@
         out_specs=[HBM, HBM],
         scratch_shapes=[pltpu.VMEM(x.shape, x.dtype) for x in arrays]
         + [pltpu.SemaphoreType.DMA((len(arrays),)), pltpu.SemaphoreType.DMA((2,))]
-        + [pltpu.VMEM(panel, F32), pltpu.VMEM(wide, F32)],
+        + [pltpu.VMEM(panel, F32), pltpu.VMEM((LANES, 2 * LANES), BF16), pltpu.VMEM(wide, F32)],
     )(*arrays)
     first = exchange(packed)
     edges = halos(air_temp)
-    air, heat, own, packed = call(
-        mid_kernel,
-        "first_step",
-        [block, panel, narrow, narrow],
+    enthalpy, heat, surface = call(
+        mid_sums_kernel,
+        "first_sums",
+        [panel, block, (2 * PAIRS, LANES)],
         32,
-        out_specs=[VMEM, VMEM, VMEM, HBM],
-        scratch_shapes=[pltpu.VMEM(panel, F32), pltpu.SemaphoreType.DMA((1,))],
-    )(
-        kept, first, air_temp, velocity, fluid, enthalpy, adjacency_lists, cells, nodes, *edges
-    )
+        scratch_shapes=[pltpu.VMEM(panel, F32)],
+    )(kept, first, enthalpy, adjacency_lists, cells, nodes)
+    air, own, packed = call(
+        mid_air_kernel,
+        "first_air",
+        [block, narrow, narrow],
+        32,
+        out_specs=[VMEM, VMEM, HBM],
+        scratch_shapes=[
+            pltpu.VMEM((LANES, 2 * LANES), BF16),
+            pltpu.SemaphoreType.DMA((1,)),
+        ],
+    )(kept, heat, surface, air_temp, velocity, fluid, cells, *edges)
     received = exchange(packed)
     edges = halos(air)
-    air, heat = call(post_kernel, "second_step", [block, panel], 32)(
-        kept, own, received, first, air, velocity, fluid, heat, adjacency_lists, cells, nodes,
-        *edges,
-    )
-    return air, heat
+    enthalpy, heat = call(post_sums_kernel, "second_sums", [panel, block], 32)(
+        kept, own, received, first, enthalpy, adjacency_lists, cells, nodes
+    )
+    (air,) = call(post_air_kernel, "second_air", [block], 32)(heat, air, velocity, fluid, *edges)
+    return air, enthalpy
 
 
 def solution(mesh):

time: 74.5 us -> 67.2 us (0.902)
  Pallas kernels: 31.5 us -> 26.9 us
  starting transfers between devices: 32.7 us -> 30.8 us
    ppermute x4, waiting for transfers between devices: 8.57 us -> 0.01 us  [halos(): out.append(lax.ppermute(tail, axis, ring))]
    all_to_all x2, waiting for transfers between devices: 0.48 us -> 8.34 us  [exchange(): lax.all_to_all(both, ('len', 'hgt'), split_axis=0, concat_axis=0, tiled=T...]
    pallas_call x1, Pallas kernels: 7.89 us -> 5.04 us  [local(): call(pre_kernel, 'pack_first', [wide, wide], 60, in_specs=[HBM] * len(arr...]
    all_to_all x2, starting transfers between devices: 18.1 us -> 16.2 us  [exchange(): lax.all_to_all(both, ('len', 'hgt'), split_axis=0, concat_axis=0, tiled=T...]
    pallas_call x2 -> x4, Pallas kernels: 23.6 us -> 21.9 us  [the longest x1 9.09 us: local(): call(post_sums_kernel, 'second_sums', [panel, block], 32)]
  transfers between devices with their start and end apart: 10 -> 10, of which waited for: 3 -> 2; matrix products, arithmetic and copies ran while one was open for 0% -> 0% of each run, Pallas kernels for 0% -> 27%
where the time goes in v3:
time: 67.2 us; the launch traced here: 67 us
  starting transfers between devices  30.8 us (46%)
  Pallas kernels  26.9 us (40%)
  waiting for transfers between devices  8.36 us (12%)
  between operations  0.84 us (1%)
    all_to_all x2, starting transfers between devices, exchange(): lax.all_to_all(both, ('len', 'hgt'), split_axis=0, concat_axis=0, tiled=T...  16.2 us
    ppermute x4, starting transfers between devices, halos(): out.append(lax.ppermute(head, axis, [(j, i) for i, j in ring]))  12.3 us
    pallas_call x1, Pallas kernels, local(): call(post_sums_kernel, 'second_sums', [panel, block], 32)  9.09 us
    pallas_call x1, Pallas kernels, local(): call(mid_sums_kernel, 'first_sums', [panel, block, (2 * PAIRS, LANES)], 3...  8.68 us
    all_to_all x2, waiting for transfers between devices, exchange(): lax.all_to_all(both, ('len', 'hgt'), split_axis=0, concat_axis=0, tiled=T...  8.34 us
    pallas_call x1, Pallas kernels, local(): call(pre_kernel, 'pack_first', [wide, wide], 60, in_specs=[HBM] * len(arr...  5.04 us
    pallas_call x1, Pallas kernels, local(): call(mid_air_kernel, 'first_air', [block, narrow, narrow], 32, out_specs=...  3.34 us
    ppermute x4, starting transfers between devices, halos(): out.append(lax.ppermute(tail, axis, ring))  2.32 us
  transfers between devices with their start and end apart: 10, of which 2 were waited for; matrix products, arithmetic and copies ran while one was open for 0% of the time, Pallas kernels for 27%

profile of v3, /device:TPU:1, one launch (start us, length us, event | category | flops | bytes accessed | tf_op | source)
XLA Modules:
  0.0 67.0 jit_solution(14381736661260162248)
XLA Ops:
  0.6 0.0 copy-start.4
  0.6 5.0 %pack_first.1 = (f32[768,128]{1,0:T(8,128)}, f32[768,128]{1,0:T(8,128)}) custom-call(f32[8,8,256]{2,1,0:T(8,128)} %air_ref.1, f32[32,128]{1,0:T(8,128)} %enthalpy_ref.1, s32[128,256]{1,0:T(8,128)} %bitcast.9, f32[128,256]{1,0:T(8,128)} %bitcast.18, s32[1,128]{1,0:T(1,128)} %rows_in.1, s32[128,256]{1,0:T(8,128)} %bitcast.13), custom_call_target="tpu_custom_call" | custom-call | tf_op jit(solution)/shard_map/pack_first/pallas_call | solution.py:397
  5.7 0.0 copy-start
  5.7 0.0 copy-start.1
  5.7 0.0 copy-start.2
  5.7 0.0 copy-start.3
  5.7 11.5 %all-to-all-start = ((f32[128,1,768]{2,1,0:T(1,128)}), f32[128,1,768]{2,1,0:T(1,128)S(1)}, u32[]{:S(2)}, u32[]{:S(2)}) async-start(f32[128,1,768]{2,1,0:T(1,128)} %bitcast.17), calls=%async_computation | async-start | bytes 786432 | tf_op jit(solution)/shard_map/all_to_all | solution.py:386
  17.2 0.0 copy-done.4
  17.3 5.5 %collective-permute-start.3 = (f32[8,1,256]{2,1,0:T(1,128)S(1)}, f32[8,1,256]{2,1,0:T(1,128)S(1)}, u32[]{:S(2)}, u32[]{:S(2)}) collective-permute-start(f32[8,1,256]{2,1,0:T(1,128)S(1)} %get-tuple-element.26), channel_id=1, source_target_pairs={{1,0},{2,1},{3,2},{4,3},{5,4},{6,5},{7,6},{8,7},{9,8},{10,9},{11,1... | collective-permute-start | bytes 24584 | tf_op jit(solution)/shard_map/ppermute | solution.py:380
  22.8 0.0 copy-start.7
  22.8 0.0 collective-permute-start.2
  22.8 0.6 collective-permute-start.1
  23.4 1.2 %collective-permute-start = (f32[1,8,256]{2,1,0:T(8,128)S(1)}, f32[1,8,256]{2,1,0:T(8,128)S(1)}, u32[]{:S(2)}, u32[]{:S(2)}) collective-permute-start(f32[1,8,256]{2,1,0:T(8,128)S(1)} %get-tuple-element.29), channel_id=1, source_target_pairs={{0,16},{16,32},{32,48},{48,64},{64,80},{80,96},{96,112},{112,0},{1... | collective-permute-start | bytes 24584 | tf_op jit(solution)/shard_map/ppermute | solution.py:379
  24.6 4.8 %all-to-all-done = f32[128,1,768]{2,1,0:T(1,128)S(1)} async-done(((f32[128,1,768]{2,1,0:T(1,128)}), f32[128,1,768]{2,1,0:T(1,128)S(1)}, u32[]{:S(2)}, u32[]{:S(2)}) %all-to-all-start) | async-done | bytes 393248 | tf_op jit(solution)/shard_map/all_to_all | solution.py:386
  29.4 0.0 copy-done
  29.4 0.0 copy-done.1
  29.4 0.0 copy-done.2
  29.4 0.0 copy-done.3
  29.4 0.0 copy-done.7
  29.4 0.0 copy-start.5
  29.4 0.0 copy-start.6
  29.4 8.7 %first_sums.1 = (f32[32,128]{1,0:T(8,128)S(1)}, f32[8,8,256]{2,1,0:T(8,128)S(1)}, f32[256,128]{1,0:T(8,128)S(1)}) custom-call(f32[768,128]{1,0:T(8,128)S(1)} %copy-done, f32[768,128]{1,0:T(8,128)S(1)} %bitcast.7, f32[32,128]{1,0:T(8,128)S(1)} %copy-done.7, s32[32,8,128]{2,1,0:T(8,128)S(1)} %copy-done.3, s32[128,256]{1,0:T(8,128)S(1)} %bitcast.10, ...), custom_call_target="tpu_custom_call" | custom-call | tf_op jit(solution)/shard_map/first_sums/pallas_call | solution.py:410
  38.1 0.0 collective-permute-done.3.right_ref
  38.1 0.0 collective-permute-done.2.left_ref
  38.1 0.0 collective-permute-done.1.ahead_ref
  38.1 0.0 collective-permute-done.behind_ref
  38.2 0.0 copy-done.5
  38.2 0.0 copy-done.6
  38.2 3.3 %first_air.1 = (f32[8,8,256]{2,1,0:T(8,128)S(1)}, f32[512,128]{1,0:T(8,128)S(1)}, f32[512,128]{1,0:T(8,128)}) custom-call(f32[768,128]{1,0:T(8,128)S(1)} %copy-done, f32[8,8,256]{2,1,0:T(8,128)S(1)} %get-tuple-element.14.heat_ref, f32[256,128]{1,0:T(8,128)S(1)} %get-tuple-element.15.surface_ref, f32[8,8,256]{2,1,0:T(8,128)S(1)} %copy-done.4, ...), custom_call_target="tpu_custom_call" | custom-call | tf_op jit(solution)/shard_map/first_air/pallas_call | solution.py:417
  41.5 4.7 %all-to-all-start.1 = ((f32[128,1,512]{2,1,0:T(1,128)}), f32[128,1,512]{2,1,0:T(1,128)S(1)}, u32[]{:S(2)}, u32[]{:S(2)}) async-start(f32[128,1,512]{2,1,0:T(1,128)} %bitcast.5), calls=%async_computation.1 | async-start | bytes 524288 | tf_op jit(solution)/shard_map/all_to_all | solution.py:386
  46.3 5.5 %collective-permute-start.7 = (f32[8,1,256]{2,1,0:T(1,128)S(1)}, f32[8,1,256]{2,1,0:T(1,128)S(1)}, u32[]{:S(2)}, u32[]{:S(2)}) collective-permute-start(f32[8,1,256]{2,1,0:T(1,128)S(1)} %get-tuple-element.22), channel_id=1, source_target_pairs={{1,0},{2,1},{3,2},{4,3},{5,4},{6,5},{7,6},{8,7},{9,8},{10,9},{11,1... | collective-permute-start | bytes 24584 | tf_op jit(solution)/shard_map/ppermute | solution.py:380
  51.8 0.0 collective-permute-start.6
  51.8 0.6 collective-permute-start.5
  52.4 1.2 %collective-permute-start.4 = (f32[1,8,256]{2,1,0:T(8,128)S(1)}, f32[1,8,256]{2,1,0:T(8,128)S(1)}, u32[]{:S(2)}, u32[]{:S(2)}) collective-permute-start(f32[1,8,256]{2,1,0:T(8,128)S(1)} %get-tuple-element.25), channel_id=1, source_target_pairs={{0,16},{16,32},{32,48},{48,64},{64,80},{80,96},{96,112},{112,0},{1... | collective-permute-start | bytes 24584 | tf_op jit(solution)/shard_map/ppermute | solution.py:379
  53.6 3.5 %all-to-all-done.1 = f32[128,1,512]{2,1,0:T(1,128)S(1)} async-done(((f32[128,1,512]{2,1,0:T(1,128)}), f32[128,1,512]{2,1,0:T(1,128)S(1)}, u32[]{:S(2)}, u32[]{:S(2)}) %all-to-all-start.1) | async-done | bytes 262176 | tf_op jit(solution)/shard_map/all_to_all | solution.py:386
  57.1 9.1 %second_sums.1 = (f32[32,128]{1,0:T(8,128)}, f32[8,8,256]{2,1,0:T(8,128)S(1)}) custom-call(f32[768,128]{1,0:T(8,128)S(1)} %copy-done, f32[512,128]{1,0:T(8,128)S(1)} %get-tuple-element.16.own_ref, f32[512,128]{1,0:T(8,128)S(1)} %bitcast.16, f32[768,128]{1,0:T(8,128)S(1)} %bitcast.8, f32[32,128]{1,0:T(8,128)S(1)} %get-tuple-element.18.enthalpy_ref, ...), custom_call_target="tpu_custom_call" | custom-call | tf_op jit(solution)/shard_map/second_sums/pallas_call | solution.py:430
  66.2 0.0 collective-permute-done.7.right_ref
  66.2 0.0 collective-permute-done.6.left_ref
  66.2 0.0 collective-permute-done.5.ahead_ref
  66.2 0.0 collective-permute-done.4.behind_ref
  66.2 0.8 %second_air.1 = f32[8,8,256]{2,1,0:T(8,128)} custom-call(f32[8,8,256]{2,1,0:T(8,128)S(1)} %get-tuple-element.19.heat_ref, f32[8,8,256]{2,1,0:T(8,128)S(1)} %get-tuple-element.20.air_ref, f32[8,8,256]{2,1,0:T(8,128)S(1)} %copy-done.5, s32[8,8,256]{2,1,0:T(8,128)S(1)} %copy-done.6, f32[1,8,256]{2,1,0:T(8,128)S(1)} %collective-permute-done.4.behind_ref, ...), custom_call_target="tpu_custom_call" | custom-call | tf_op jit(solution)/shard_map/second_air/pallas_call | solution.py:433
  (4 shorter events, 0.0 us)
Async XLA Ops:
  0.6 16.6 %copy-start.4 = (f32[8,8,256]{2,1,0:T(8,128)S(1)}, f32[8,8,256]{2,1,0:T(8,128)}, u32[]{:S(2)}) copy-start(f32[8,8,256]{2,1,0:T(8,128)} %air_ref.1) | copy-start | bytes 196612
  5.7 23.7 %copy-start = (f32[768,128]{1,0:T(8,128)S(1)}, f32[768,128]{1,0:T(8,128)}, u32[]{:S(2)}) copy-start(f32[768,128]{1,0:T(8,128)} %get-tuple-element.12.own_ref.kept_ref) | copy-start | bytes 1179652
  5.7 23.7 %copy-start.1 = (s32[1,128,256]{2,1,0:T(8,128)S(1)}, s32[1,128,256]{2,1,0:T(8,128)}, u32[]{:S(2)}) copy-start(s32[1,128,256]{2,1,0:T(8,128)} %param.14) | copy-start | bytes 393220
  5.7 23.7 %copy-start.2 = (s32[1,128,256]{2,1,0:T(8,128)S(1)}, s32[1,128,256]{2,1,0:T(8,128)}, u32[]{:S(2)}) copy-start(s32[1,128,256]{2,1,0:T(8,128)} %param.17) | copy-start | bytes 393220
  5.7 23.7 %copy-start.3 = (s32[32,8,128]{2,1,0:T(8,128)S(1)}, s32[32,8,128]{2,1,0:T(8,128)}, u32[]{:S(2)}) copy-start(s32[32,8,128]{2,1,0:T(8,128)} %links_ref.3) | copy-start | bytes 393220
  5.7 23.6 %all-to-all-start = ((f32[128,1,768]{2,1,0:T(1,128)}), f32[128,1,768]{2,1,0:T(1,128)S(1)}, u32[]{:S(2)}, u32[]{:S(2)}) async-start(f32[128,1,768]{2,1,0:T(1,128)} %bitcast.17), calls=%async_computation | async-start | bytes 786432 | tf_op jit(solution)/shard_map/all_to_all | solution.py:386
  17.3 20.8 %collective-permute-start.3 = (f32[8,1,256]{2,1,0:T(1,128)S(1)}, f32[8,1,256]{2,1,0:T(1,128)S(1)}, u32[]{:S(2)}, u32[]{:S(2)}) collective-permute-start(f32[8,1,256]{2,1,0:T(1,128)S(1)} %get-tuple-element.26), channel_id=1, source_target_pairs={{1,0},{2,1},{3,2},{4,3},{5,4},{6,5},{7,6},{8,7},{9,8},{10,9},{11,1... | collective-permute-start | bytes 24584 | tf_op jit(solution)/shard_map/ppermute | solution.py:380
  22.8 6.6 %copy-start.7 = (f32[32,128]{1,0:T(8,128)S(1)}, f32[32,128]{1,0:T(8,128)}, u32[]{:S(2)}) copy-start(f32[32,128]{1,0:T(8,128)} %enthalpy_ref.1) | copy-start | bytes 49156
  22.8 15.4 %collective-permute-start.2 = (f32[8,1,256]{2,1,0:T(1,128)S(1)}, f32[8,1,256]{2,1,0:T(1,128)S(1)}, u32[]{:S(2)}, u32[]{:S(2)}) collective-permute-start(f32[8,1,256]{2,1,0:T(1,128)S(1)} %get-tuple-element.27), channel_id=1, source_target_pairs={{0,1},{1,2},{2,3},{3,4},{4,5},{5,6},{6,7},{7,8},{8,9},{9,10},{10,1... | collective-permute-start | bytes 24584 | tf_op jit(solution)/shard_map/ppermute | solution.py:379
  22.8 15.4 %collective-permute-start.1 = (f32[1,8,256]{2,1,0:T(8,128)S(1)}, f32[1,8,256]{2,1,0:T(8,128)S(1)}, u32[]{:S(2)}, u32[]{:S(2)}) collective-permute-start(f32[1,8,256]{2,1,0:T(8,128)S(1)} %get-tuple-element.28), channel_id=1, source_target_pairs={{16,0},{32,16},{48,32},{64,48},{80,64},{96,80},{112,96},{0,112},{1... | collective-permute-start | bytes 24584 | tf_op jit(solution)/shard_map/ppermute | solution.py:380
  23.4 14.7 %collective-permute-start = (f32[1,8,256]{2,1,0:T(8,128)S(1)}, f32[1,8,256]{2,1,0:T(8,128)S(1)}, u32[]{:S(2)}, u32[]{:S(2)}) collective-permute-start(f32[1,8,256]{2,1,0:T(8,128)S(1)} %get-tuple-element.29), channel_id=1, source_target_pairs={{0,16},{16,32},{32,48},{48,64},{64,80},{80,96},{96,112},{112,0},{1... | collective-permute-start | bytes 24584 | tf_op jit(solution)/shard_map/ppermute | solution.py:379
  29.4 8.8 %copy-start.5 = (f32[8,8,256]{2,1,0:T(8,128)S(1)}, f32[8,8,256]{2,1,0:T(8,128)}, u32[]{:S(2)}) copy-start(f32[8,8,256]{2,1,0:T(8,128)} %velocity_ref.3) | copy-start | bytes 196612
  29.4 8.8 %copy-start.6 = (s32[8,8,256]{2,1,0:T(8,128)S(1)}, s32[8,8,256]{2,1,0:T(8,128)}, u32[]{:S(2)}) copy-start(s32[8,8,256]{2,1,0:T(8,128)} %fluid_ref.3) | copy-start | bytes 196612
  41.5 15.6 %all-to-all-start.1 = ((f32[128,1,512]{2,1,0:T(1,128)}), f32[128,1,512]{2,1,0:T(1,128)S(1)}, u32[]{:S(2)}, u32[]{:S(2)}) async-start(f32[128,1,512]{2,1,0:T(1,128)} %bitcast.5), calls=%async_computation.1 | async-start | bytes 524288 | tf_op jit(solution)/shard_map/all_to_all | solution.py:386
  46.3 20.0 %collective-permute-start.7 = (f32[8,1,256]{2,1,0:T(1,128)S(1)}, f32[8,1,256]{2,1,0:T(1,128)S(1)}, u32[]{:S(2)}, u32[]{:S(2)}) collective-permute-start(f32[8,1,256]{2,1,0:T(1,128)S(1)} %get-tuple-element.22), channel_id=1, source_target_pairs={{1,0},{2,1},{3,2},{4,3},{5,4},{6,5},{7,6},{8,7},{9,8},{10,9},{11,1... | collective-permute-start | bytes 24584 | tf_op jit(solution)/shard_map/ppermute | solution.py:380
  51.8 14.4 %collective-permute-start.6 = (f32[8,1,256]{2,1,0:T(1,128)S(1)}, f32[8,1,256]{2,1,0:T(1,128)S(1)}, u32[]{:S(2)}, u32[]{:S(2)}) collective-permute-start(f32[8,1,256]{2,1,0:T(1,128)S(1)} %get-tuple-element.23), channel_id=1, source_target_pairs={{0,1},{1,2},{2,3},{3,4},{4,5},{5,6},{6,7},{7,8},{8,9},{9,10},{10,1... | collective-permute-start | bytes 24584 | tf_op jit(solution)/shard_map/ppermute | solution.py:379
  51.8 14.4 %collective-permute-start.5 = (f32[1,8,256]{2,1,0:T(8,128)S(1)}, f32[1,8,256]{2,1,0:T(8,128)S(1)}, u32[]{:S(2)}, u32[]{:S(2)}) collective-permute-start(f32[1,8,256]{2,1,0:T(8,128)S(1)} %get-tuple-element.24), channel_id=1, source_target_pairs={{16,0},{32,16},{48,32},{64,48},{80,64},{96,80},{112,96},{0,112},{1... | collective-permute-start | bytes 24584 | tf_op jit(solution)/shard_map/ppermute | solution.py:380
  52.4 13.8 %collective-permute-start.4 = (f32[1,8,256]{2,1,0:T(8,128)S(1)}, f32[1,8,256]{2,1,0:T(8,128)S(1)}, u32[]{:S(2)}, u32[]{:S(2)}) collective-permute-start(f32[1,8,256]{2,1,0:T(8,128)S(1)} %get-tuple-element.25), channel_id=1, source_target_pairs={{0,16},{16,32},{32,48},{48,64},{64,80},{80,96},{96,112},{112,0},{1... | collective-permute-start | bytes 24584 | tf_op jit(solution)/shard_map/ppermute | solution.py:379

commit v4 on v3

--- a/solution.py
+++ b/solution.py
@@ -67,11 +67,13 @@
 
 
 def one_hot(index, count, iota):
+    return one_hot_of(index, [iota + BF16(16 * i) for i in range(count // 16)])
+
+
+def one_hot_of(index, marks):
     one = jnp.ones((16, LANES), BF16)
     zero = jnp.zeros((16, LANES), BF16)
-    return jnp.concatenate(
-        [jnp.where(index == iota + BF16(16 * i), one, zero) for i in range(count // 16)], axis=0
-    )
+    return jnp.concatenate([jnp.where(index == mark, one, zero) for mark in marks], axis=0)
 
 
 def weighted(index, values, count, iota):
@@ -82,28 +84,33 @@
     )
 
 
-def product(rows, high_count, iota):
+def product(rows, high_count, low_count, iota):
     left = jnp.concatenate(
         [weighted(as_bf16(high), values, high_count, iota) for high, _, values in rows], axis=1
     )
-    right = jnp.concatenate([one_hot(as_bf16(low), LANES, iota) for _, low, _ in rows], axis=1)
+    right = jnp.concatenate([one_hot(as_bf16(low), low_count, iota) for _, low, _ in rows], axis=1)
     return lax.dot_general(left, right, (((1,), (1,)), ((), ())), preferred_element_type=F32)
 
 
-def scatter(row_of, high_count, group, beside=None):
+def scatter(row_of, split, beside=None, group=64):
     iota = iota16()
-
-    def body(g, acc):
+    high_count, low_count, digits = split
+
+    def body(g, total):
         start = pl.multiple_of(g * group, group)
-        acc = acc + product(
-            [row_of((start, k), half) for k in range(group) for half in range(2)], high_count, iota
-        )
+        for at in range(0, group, 8):
+            rows = []
+            for k in range(at, at + 8):
+                for half in range(2):
+                    index, value = row_of((start, k), half)
+                    rows.append(digits(index) + ([value],))
+            total = total + product(rows, high_count, low_count, iota)
         if beside is not None:
-            beside(start)
-        return acc
-
-    acc = lax.fori_loop(0, PAIRS // group, body, jnp.zeros((2 * high_count, LANES), F32))
-    return acc[:high_count] + acc[high_count:]
+            beside(start, group)
+        return total
+
+    total = lax.fori_loop(0, PAIRS // group, body, jnp.zeros((2 * high_count, low_count), F32))
+    return total[:high_count] + total[high_count:]
 
 
 def lane_row(ref, row):
@@ -120,8 +127,8 @@
     return ((cell >> 7) & 1) * 64 + (cell >> 8), cell & (LANES - 1)
 
 
-def node_split(node):
-    return node >> 7, node & (LANES - 1)
+CELL_SPLIT = (128, 128, cell_split)
+NODE_SPLIT = (64, 64, lambda node: (((node >> 6) & 1) * 32 + (node >> 7), node & 63))
 
 
 def to_block(table):
@@ -140,13 +147,14 @@
 
 def gather_by_product(table, cells):
     iota = iota16()
+    marks = [iota + iota + BF16(32 * i + half) for half in range(2) for i in range(4)]
     count = lax.broadcasted_iota(I32, (8, LANES), 0)
     hots, lows = [], []
     for cell in cells:
         for k in range(8):
-            high, low = cell_split(jnp.broadcast_to(cell[k : k + 1], (16, LANES)))
-            hots.append(one_hot(as_bf16(high), LANES, iota))
-            lows.append(low[:8])
+            row = cell[k : k + 1]
+            hots.append(one_hot_of(as_bf16(jnp.broadcast_to(row >> 7, (16, LANES))), marks))
+            lows.append(jnp.broadcast_to(row, (8, LANES)))
     hots = jnp.concatenate(hots, axis=1)
     found = lax.dot_general(
         table,
@@ -159,7 +167,7 @@
         column = found[:, n * LANES : (n + 1) * LANES]
         level = [column[k : k + 8] for k in range(0, LANES, 8)]
         for b in range(3, 7):
-            bit = ((low >> b) & 1) == 1
+            bit = (low & (1 << b)) != 0
             level = [jnp.where(bit, y, x) for x, y in zip(level[::2], level[1::2])]
         rows.append(
             jnp.sum(jnp.where((low & 7) == count, level[0], 0.0), axis=0, keepdims=True)
@@ -271,9 +279,9 @@
         base = p * per_pair + half
         heat = lane_row(first_ref, p * 6 + 4 + half) * lane_row(received_ref, base + 2)
         heat = heat - lane_row(own_ref, base)
-        return cell_split(pair_row(cell_ref, pair, half)) + ([heat],)
-
-    heat_ref[...] = to_block(scatter(heat_row, 128, 32, beside))
+        return pair_row(cell_ref, pair, half), heat
+
+    heat_ref[...] = to_block(scatter(heat_row, CELL_SPLIT, beside))
 
 
 def air_part(heat_ref, air_ref, velocity_ref, fluid_ref, edge_refs, air_out_ref):
@@ -293,9 +301,10 @@
         base = p * per_pair + half
         heat = lane_row(first_ref, p * 6 + 4 + half) * lane_row(own_ref, base + 2)
         heat = lane_row(received_ref, base) - heat
-        return node_split(pair_row(node_ref, pair, half)) + ([heat],)
-
-    gained = scatter(node_row, 32, 32)
+        return pair_row(node_ref, pair, half), heat
+
+    gained = scatter(node_row, NODE_SPLIT)
+    gained = jnp.concatenate([gained[:32], gained[32:]], axis=1)
     enthalpy = enthalpy_ref[...]
     return enthalpy + DT_NODE * (conduction(node_temp(enthalpy), links_ref) + gained)
 
@@ -309,7 +318,9 @@
     warmth_ref[...] = node_temp(enthalpy)
     heat_part(
         own_ref, first_ref, own_ref, 6, cell_ref, heat_ref,
-        lambda start: pack_nodes(warmth_ref, node_ref, surface_ref, 2, 0, start, 32),
+        lambda start, count: pack_nodes(
+            warmth_ref, node_ref, surface_ref, 2, 0, start, count
+        ),
     )
 
 

time: 67.2 us -> 64.5 us (0.960)
  Pallas kernels: 26.9 us -> 24.2 us
    pallas_call x1, Pallas kernels: 9.09 us -> 7.73 us  [local(): call(post_sums_kernel, 'second_sums', [panel, block], 32)]
    pallas_call x1, Pallas kernels: 8.68 us -> 7.31 us  [local(): call(mid_sums_kernel, 'first_sums', [panel, block, (2 * PAIRS, LANES)], 3...]
  transfers between devices with their start and end apart: 10 -> 10, of which waited for: 2 -> 2; matrix products, arithmetic and copies ran while one was open for 0% -> 0% of each run, Pallas kernels for 27% -> 23%
where the time goes in v4:
time: 64.5 us; the launch traced here: 64.3 us
  starting transfers between devices  30.8 us (48%)
  Pallas kernels  24.2 us (38%)
  waiting for transfers between devices  8.36 us (13%)
  between operations  0.84 us (1%)
    all_to_all x2, starting transfers between devices, exchange(): lax.all_to_all(both, ('len', 'hgt'), split_axis=0, concat_axis=0, tiled=T...  16.2 us
    ppermute x4, starting transfers between devices, halos(): out.append(lax.ppermute(head, axis, [(j, i) for i, j in ring]))  12.3 us
    all_to_all x2, waiting for transfers between devices, exchange(): lax.all_to_all(both, ('len', 'hgt'), split_axis=0, concat_axis=0, tiled=T...  8.34 us
    pallas_call x1, Pallas kernels, local(): call(post_sums_kernel, 'second_sums', [panel, block], 32)  7.73 us
    pallas_call x1, Pallas kernels, local(): call(mid_sums_kernel, 'first_sums', [panel, block, (2 * PAIRS, LANES)], 3...  7.31 us
    pallas_call x1, Pallas kernels, local(): call(pre_kernel, 'pack_first', [wide, wide], 60, in_specs=[HBM] * len(arr...  5.04 us
    pallas_call x1, Pallas kernels, local(): call(mid_air_kernel, 'first_air', [block, narrow, narrow], 32, out_specs=...  3.37 us
    ppermute x4, starting transfers between devices, halos(): out.append(lax.ppermute(tail, axis, ring))  2.32 us
  transfers between devices with their start and end apart: 10, of which 2 were waited for; matrix products, arithmetic and copies ran while one was open for 0% of the time, Pallas kernels for 23%

profile of v4, /device:TPU:1, one launch (start us, length us, event | category | flops | bytes accessed | tf_op | source)
XLA Modules:
  0.0 64.3 jit_solution(17860781697686265071)
XLA Ops:
  0.6 0.0 copy-start.4
  0.6 5.0 %pack_first.1 = (f32[768,128]{1,0:T(8,128)}, f32[768,128]{1,0:T(8,128)}) custom-call(f32[8,8,256]{2,1,0:T(8,128)} %air_ref.1, f32[32,128]{1,0:T(8,128)} %enthalpy_ref.1, s32[128,256]{1,0:T(8,128)} %bitcast.9, f32[128,256]{1,0:T(8,128)} %bitcast.18, s32[1,128]{1,0:T(1,128)} %rows_in.1, s32[128,256]{1,0:T(8,128)} %bitcast.13), custom_call_target="tpu_custom_call" | custom-call | tf_op jit(solution)/shard_map/pack_first/pallas_call | solution.py:408
  5.7 0.0 copy-start
  5.7 0.0 copy-start.1
  5.7 0.0 copy-start.2
  5.7 0.0 copy-start.3
  5.7 11.5 %all-to-all-start = ((f32[128,1,768]{2,1,0:T(1,128)}), f32[128,1,768]{2,1,0:T(1,128)S(1)}, u32[]{:S(2)}, u32[]{:S(2)}) async-start(f32[128,1,768]{2,1,0:T(1,128)} %bitcast.17), calls=%async_computation | async-start | bytes 786432 | tf_op jit(solution)/shard_map/all_to_all | solution.py:397
  17.2 0.0 copy-done.4
  17.3 5.5 %collective-permute-start.3 = (f32[8,1,256]{2,1,0:T(1,128)S(1)}, f32[8,1,256]{2,1,0:T(1,128)S(1)}, u32[]{:S(2)}, u32[]{:S(2)}) collective-permute-start(f32[8,1,256]{2,1,0:T(1,128)S(1)} %get-tuple-element.26), channel_id=1, source_target_pairs={{1,0},{2,1},{3,2},{4,3},{5,4},{6,5},{7,6},{8,7},{9,8},{10,9},{11,1... | collective-permute-start | bytes 24584 | tf_op jit(solution)/shard_map/ppermute | solution.py:391
  22.8 0.0 copy-start.7
  22.8 0.0 collective-permute-start.2
  22.8 0.6 %collective-permute-start.1 = (f32[1,8,256]{2,1,0:T(8,128)S(1)}, f32[1,8,256]{2,1,0:T(8,128)S(1)}, u32[]{:S(2)}, u32[]{:S(2)}) collective-permute-start(f32[1,8,256]{2,1,0:T(8,128)S(1)} %get-tuple-element.28), channel_id=1, source_target_pairs={{16,0},{32,16},{48,32},{64,48},{80,64},{96,80},{112,96},{0,112},{1... | collective-permute-start | bytes 24584 | tf_op jit(solution)/shard_map/ppermute | solution.py:391
  23.4 1.2 %collective-permute-start = (f32[1,8,256]{2,1,0:T(8,128)S(1)}, f32[1,8,256]{2,1,0:T(8,128)S(1)}, u32[]{:S(2)}, u32[]{:S(2)}) collective-permute-start(f32[1,8,256]{2,1,0:T(8,128)S(1)} %get-tuple-element.29), channel_id=1, source_target_pairs={{0,16},{16,32},{32,48},{48,64},{64,80},{80,96},{96,112},{112,0},{1... | collective-permute-start | bytes 24584 | tf_op jit(solution)/shard_map/ppermute | solution.py:390
  24.6 4.8 %all-to-all-done = f32[128,1,768]{2,1,0:T(1,128)S(1)} async-done(((f32[128,1,768]{2,1,0:T(1,128)}), f32[128,1,768]{2,1,0:T(1,128)S(1)}, u32[]{:S(2)}, u32[]{:S(2)}) %all-to-all-start) | async-done | bytes 393248 | tf_op jit(solution)/shard_map/all_to_all | solution.py:397
  29.4 0.0 copy-done
  29.4 0.0 copy-done.1
  29.4 0.0 copy-done.2
  29.4 0.0 copy-done.3
  29.4 0.0 copy-done.7
  29.4 0.0 copy-start.5
  29.4 0.0 copy-start.6
  29.4 7.3 %first_sums.1 = (f32[32,128]{1,0:T(8,128)S(1)}, f32[8,8,256]{2,1,0:T(8,128)S(1)}, f32[256,128]{1,0:T(8,128)S(1)}) custom-call(f32[768,128]{1,0:T(8,128)S(1)} %copy-done, f32[768,128]{1,0:T(8,128)S(1)} %bitcast.7, f32[32,128]{1,0:T(8,128)S(1)} %copy-done.7, s32[32,8,128]{2,1,0:T(8,128)S(1)} %copy-done.3, s32[128,256]{1,0:T(8,128)S(1)} %bitcast.10, ...), custom_call_target="tpu_custom_call" | custom-call | tf_op jit(solution)/shard_map/first_sums/pallas_call | solution.py:421
  36.7 0.0 collective-permute-done.3.right_ref
  36.8 0.0 collective-permute-done.2.left_ref
  36.8 0.0 collective-permute-done.1.ahead_ref
  36.8 0.0 collective-permute-done.behind_ref
  36.8 0.0 copy-done.5
  36.8 0.0 copy-done.6
  36.8 3.4 %first_air.1 = (f32[8,8,256]{2,1,0:T(8,128)S(1)}, f32[512,128]{1,0:T(8,128)S(1)}, f32[512,128]{1,0:T(8,128)}) custom-call(f32[768,128]{1,0:T(8,128)S(1)} %copy-done, f32[8,8,256]{2,1,0:T(8,128)S(1)} %get-tuple-element.14.heat_ref, f32[256,128]{1,0:T(8,128)S(1)} %get-tuple-element.15.surface_ref, f32[8,8,256]{2,1,0:T(8,128)S(1)} %copy-done.4, ...), custom_call_target="tpu_custom_call" | custom-call | tf_op jit(solution)/shard_map/first_air/pallas_call | solution.py:428
  40.2 4.7 %all-to-all-start.1 = ((f32[128,1,512]{2,1,0:T(1,128)}), f32[128,1,512]{2,1,0:T(1,128)S(1)}, u32[]{:S(2)}, u32[]{:S(2)}) async-start(f32[128,1,512]{2,1,0:T(1,128)} %bitcast.5), calls=%async_computation.1 | async-start | bytes 524288 | tf_op jit(solution)/shard_map/all_to_all | solution.py:397
  44.9 5.5 %collective-permute-start.7 = (f32[8,1,256]{2,1,0:T(1,128)S(1)}, f32[8,1,256]{2,1,0:T(1,128)S(1)}, u32[]{:S(2)}, u32[]{:S(2)}) collective-permute-start(f32[8,1,256]{2,1,0:T(1,128)S(1)} %get-tuple-element.22), channel_id=1, source_target_pairs={{1,0},{2,1},{3,2},{4,3},{5,4},{6,5},{7,6},{8,7},{9,8},{10,9},{11,1... | collective-permute-start | bytes 24584 | tf_op jit(solution)/shard_map/ppermute | solution.py:391
  50.4 0.0 collective-permute-start.6
  50.5 0.6 collective-permute-start.5
  51.1 1.2 %collective-permute-start.4 = (f32[1,8,256]{2,1,0:T(8,128)S(1)}, f32[1,8,256]{2,1,0:T(8,128)S(1)}, u32[]{:S(2)}, u32[]{:S(2)}) collective-permute-start(f32[1,8,256]{2,1,0:T(8,128)S(1)} %get-tuple-element.25), channel_id=1, source_target_pairs={{0,16},{16,32},{32,48},{48,64},{64,80},{80,96},{96,112},{112,0},{1... | collective-permute-start | bytes 24584 | tf_op jit(solution)/shard_map/ppermute | solution.py:390
  52.2 3.5 %all-to-all-done.1 = f32[128,1,512]{2,1,0:T(1,128)S(1)} async-done(((f32[128,1,512]{2,1,0:T(1,128)}), f32[128,1,512]{2,1,0:T(1,128)S(1)}, u32[]{:S(2)}, u32[]{:S(2)}) %all-to-all-start.1) | async-done | bytes 262176 | tf_op jit(solution)/shard_map/all_to_all | solution.py:397
  55.8 7.7 %second_sums.1 = (f32[32,128]{1,0:T(8,128)}, f32[8,8,256]{2,1,0:T(8,128)S(1)}) custom-call(f32[768,128]{1,0:T(8,128)S(1)} %copy-done, f32[512,128]{1,0:T(8,128)S(1)} %get-tuple-element.16.own_ref, f32[512,128]{1,0:T(8,128)S(1)} %bitcast.16, f32[768,128]{1,0:T(8,128)S(1)} %bitcast.8, f32[32,128]{1,0:T(8,128)S(1)} %get-tuple-element.18.enthalpy_ref, ...), custom_call_target="tpu_custom_call" | custom-call | tf_op jit(solution)/shard_map/second_sums/pallas_call | solution.py:441
  63.5 0.0 collective-permute-done.7.right_ref
  63.5 0.0 collective-permute-done.6.left_ref
  63.5 0.0 collective-permute-done.5.ahead_ref
  63.5 0.0 collective-permute-done.4.behind_ref
  63.5 0.8 %second_air.1 = f32[8,8,256]{2,1,0:T(8,128)} custom-call(f32[8,8,256]{2,1,0:T(8,128)S(1)} %get-tuple-element.19.heat_ref, f32[8,8,256]{2,1,0:T(8,128)S(1)} %get-tuple-element.20.air_ref, f32[8,8,256]{2,1,0:T(8,128)S(1)} %copy-done.5, s32[8,8,256]{2,1,0:T(8,128)S(1)} %copy-done.6, f32[1,8,256]{2,1,0:T(8,128)S(1)} %collective-permute-done.4.behind_ref, ...), custom_call_target="tpu_custom_call" | custom-call | tf_op jit(solution)/shard_map/second_air/pallas_call | solution.py:444
  (4 shorter events, 0.0 us)
Async XLA Ops:
  0.6 16.6 %copy-start.4 = (f32[8,8,256]{2,1,0:T(8,128)S(1)}, f32[8,8,256]{2,1,0:T(8,128)}, u32[]{:S(2)}) copy-start(f32[8,8,256]{2,1,0:T(8,128)} %air_ref.1) | copy-start | bytes 196612
  5.7 23.7 %copy-start = (f32[768,128]{1,0:T(8,128)S(1)}, f32[768,128]{1,0:T(8,128)}, u32[]{:S(2)}) copy-start(f32[768,128]{1,0:T(8,128)} %get-tuple-element.12.own_ref.kept_ref) | copy-start | bytes 1179652
  5.7 23.7 %copy-start.1 = (s32[1,128,256]{2,1,0:T(8,128)S(1)}, s32[1,128,256]{2,1,0:T(8,128)}, u32[]{:S(2)}) copy-start(s32[1,128,256]{2,1,0:T(8,128)} %param.14) | copy-start | bytes 393220
  5.7 23.7 %copy-start.2 = (s32[1,128,256]{2,1,0:T(8,128)S(1)}, s32[1,128,256]{2,1,0:T(8,128)}, u32[]{:S(2)}) copy-start(s32[1,128,256]{2,1,0:T(8,128)} %param.17) | copy-start | bytes 393220
  5.7 23.7 %copy-start.3 = (s32[32,8,128]{2,1,0:T(8,128)S(1)}, s32[32,8,128]{2,1,0:T(8,128)}, u32[]{:S(2)}) copy-start(s32[32,8,128]{2,1,0:T(8,128)} %links_ref.3) | copy-start | bytes 393220
  5.7 23.6 %all-to-all-start = ((f32[128,1,768]{2,1,0:T(1,128)}), f32[128,1,768]{2,1,0:T(1,128)S(1)}, u32[]{:S(2)}, u32[]{:S(2)}) async-start(f32[128,1,768]{2,1,0:T(1,128)} %bitcast.17), calls=%async_computation | async-start | bytes 786432 | tf_op jit(solution)/shard_map/all_to_all | solution.py:397
  17.3 19.5 %collective-permute-start.3 = (f32[8,1,256]{2,1,0:T(1,128)S(1)}, f32[8,1,256]{2,1,0:T(1,128)S(1)}, u32[]{:S(2)}, u32[]{:S(2)}) collective-permute-start(f32[8,1,256]{2,1,0:T(1,128)S(1)} %get-tuple-element.26), channel_id=1, source_target_pairs={{1,0},{2,1},{3,2},{4,3},{5,4},{6,5},{7,6},{8,7},{9,8},{10,9},{11,1... | collective-permute-start | bytes 24584 | tf_op jit(solution)/shard_map/ppermute | solution.py:391
  22.8 6.6 %copy-start.7 = (f32[32,128]{1,0:T(8,128)S(1)}, f32[32,128]{1,0:T(8,128)}, u32[]{:S(2)}) copy-start(f32[32,128]{1,0:T(8,128)} %enthalpy_ref.1) | copy-start | bytes 49156
  22.8 14.0 %collective-permute-start.2 = (f32[8,1,256]{2,1,0:T(1,128)S(1)}, f32[8,1,256]{2,1,0:T(1,128)S(1)}, u32[]{:S(2)}, u32[]{:S(2)}) collective-permute-start(f32[8,1,256]{2,1,0:T(1,128)S(1)} %get-tuple-element.27), channel_id=1, source_target_pairs={{0,1},{1,2},{2,3},{3,4},{4,5},{5,6},{6,7},{7,8},{8,9},{9,10},{10,1... | collective-permute-start | bytes 24584 | tf_op jit(solution)/shard_map/ppermute | solution.py:390
  22.8 14.0 %collective-permute-start.1 = (f32[1,8,256]{2,1,0:T(8,128)S(1)}, f32[1,8,256]{2,1,0:T(8,128)S(1)}, u32[]{:S(2)}, u32[]{:S(2)}) collective-permute-start(f32[1,8,256]{2,1,0:T(8,128)S(1)} %get-tuple-element.28), channel_id=1, source_target_pairs={{16,0},{32,16},{48,32},{64,48},{80,64},{96,80},{112,96},{0,112},{1... | collective-permute-start | bytes 24584 | tf_op jit(solution)/shard_map/ppermute | solution.py:391
  23.4 13.4 %collective-permute-start = (f32[1,8,256]{2,1,0:T(8,128)S(1)}, f32[1,8,256]{2,1,0:T(8,128)S(1)}, u32[]{:S(2)}, u32[]{:S(2)}) collective-permute-start(f32[1,8,256]{2,1,0:T(8,128)S(1)} %get-tuple-element.29), channel_id=1, source_target_pairs={{0,16},{16,32},{32,48},{48,64},{64,80},{80,96},{96,112},{112,0},{1... | collective-permute-start | bytes 24584 | tf_op jit(solution)/shard_map/ppermute | solution.py:390
  29.4 7.4 %copy-start.5 = (f32[8,8,256]{2,1,0:T(8,128)S(1)}, f32[8,8,256]{2,1,0:T(8,128)}, u32[]{:S(2)}) copy-start(f32[8,8,256]{2,1,0:T(8,128)} %velocity_ref.3) | copy-start | bytes 196612
  29.4 7.4 %copy-start.6 = (s32[8,8,256]{2,1,0:T(8,128)S(1)}, s32[8,8,256]{2,1,0:T(8,128)}, u32[]{:S(2)}) copy-start(s32[8,8,256]{2,1,0:T(8,128)} %fluid_ref.3) | copy-start | bytes 196612
  40.2 15.6 %all-to-all-start.1 = ((f32[128,1,512]{2,1,0:T(1,128)}), f32[128,1,512]{2,1,0:T(1,128)S(1)}, u32[]{:S(2)}, u32[]{:S(2)}) async-start(f32[128,1,512]{2,1,0:T(1,128)} %bitcast.5), calls=%async_computation.1 | async-start | bytes 524288 | tf_op jit(solution)/shard_map/all_to_all | solution.py:397
  44.9 18.6 %collective-permute-start.7 = (f32[8,1,256]{2,1,0:T(1,128)S(1)}, f32[8,1,256]{2,1,0:T(1,128)S(1)}, u32[]{:S(2)}, u32[]{:S(2)}) collective-permute-start(f32[8,1,256]{2,1,0:T(1,128)S(1)} %get-tuple-element.22), channel_id=1, source_target_pairs={{1,0},{2,1},{3,2},{4,3},{5,4},{6,5},{7,6},{8,7},{9,8},{10,9},{11,1... | collective-permute-start | bytes 24584 | tf_op jit(solution)/shard_map/ppermute | solution.py:391
  50.4 13.1 %collective-permute-start.6 = (f32[8,1,256]{2,1,0:T(1,128)S(1)}, f32[8,1,256]{2,1,0:T(1,128)S(1)}, u32[]{:S(2)}, u32[]{:S(2)}) collective-permute-start(f32[8,1,256]{2,1,0:T(1,128)S(1)} %get-tuple-element.23), channel_id=1, source_target_pairs={{0,1},{1,2},{2,3},{3,4},{4,5},{5,6},{6,7},{7,8},{8,9},{9,10},{10,1... | collective-permute-start | bytes 24584 | tf_op jit(solution)/shard_map/ppermute | solution.py:390
  50.5 13.1 %collective-permute-start.5 = (f32[1,8,256]{2,1,0:T(8,128)S(1)}, f32[1,8,256]{2,1,0:T(8,128)S(1)}, u32[]{:S(2)}, u32[]{:S(2)}) collective-permute-start(f32[1,8,256]{2,1,0:T(8,128)S(1)} %get-tuple-element.24), channel_id=1, source_target_pairs={{16,0},{32,16},{48,32},{64,48},{80,64},{96,80},{112,96},{0,112},{1... | collective-permute-start | bytes 24584 | tf_op jit(solution)/shard_map/ppermute | solution.py:391
  51.1 12.4 %collective-permute-start.4 = (f32[1,8,256]{2,1,0:T(8,128)S(1)}, f32[1,8,256]{2,1,0:T(8,128)S(1)}, u32[]{:S(2)}, u32[]{:S(2)}) collective-permute-start(f32[1,8,256]{2,1,0:T(8,128)S(1)} %get-tuple-element.25), channel_id=1, source_target_pairs={{0,16},{16,32},{32,48},{48,64},{64,80},{80,96},{96,112},{112,0},{1... | collective-permute-start | bytes 24584 | tf_op jit(solution)/shard_map/ppermute | solution.py:390

commit v5 on v4

--- a/solution.py
+++ b/solution.py
@@ -92,7 +92,7 @@
     return lax.dot_general(left, right, (((1,), (1,)), ((), ())), preferred_element_type=F32)
 
 
-def scatter(row_of, split, beside=None, group=64):
+def scatter(row_of, split, beside=None, group=128):
     iota = iota16()
     high_count, low_count, digits = split
 
@@ -248,12 +248,14 @@
     wait_out(own_ref, (packed_out, kept_out), out_sems)
 
 
-def conduction(warmth, links_ref):
-    rows = []
-    for b in range(warmth.shape[0]):
-        linked = take(warmth[b : b + 1], links_ref[b])
-        rows.append(jnp.sum(linked, axis=0, keepdims=True))
-    return jnp.concatenate(rows, axis=0) - 8.0 * warmth
+def conduct(warmth_ref, links_ref, conducted_ref, start, count):
+    blocks = warmth_ref.shape[0] * count // PAIRS
+    first = start // count * blocks
+    for k in range(blocks):
+        at = pl.ds(first + k, 1)
+        warmth = warmth_ref[at, :]
+        linked = take(warmth, links_ref[first + k])
+        conducted_ref[at, :] = jnp.sum(linked, axis=0, keepdims=True) - 8.0 * warmth
 
 
 def air_step(air, velocity, fluid, behind_halo, ahead_halo, left_halo, right_halo, source):
@@ -295,7 +297,10 @@
     )
 
 
-def node_part(own_ref, received_ref, first_ref, per_pair, enthalpy_ref, links_ref, node_ref):
+def node_part(
+    own_ref, received_ref, first_ref, per_pair, enthalpy_ref, links_ref, node_ref, warmth_ref,
+    conducted_ref,
+):
     def node_row(pair, half):
         p = pair[0] + pair[1]
         base = p * per_pair + half
@@ -303,17 +308,25 @@
         heat = lane_row(received_ref, base) - heat
         return pair_row(node_ref, pair, half), heat
 
-    gained = scatter(node_row, NODE_SPLIT)
+    enthalpy = enthalpy_ref[...]
+    warmth_ref[...] = node_temp(enthalpy)
+    gained = scatter(
+        node_row,
+        NODE_SPLIT,
+        lambda start, count: conduct(warmth_ref, links_ref, conducted_ref, start, count),
+    )
     gained = jnp.concatenate([gained[:32], gained[32:]], axis=1)
-    enthalpy = enthalpy_ref[...]
-    return enthalpy + DT_NODE * (conduction(node_temp(enthalpy), links_ref) + gained)
+    return enthalpy + DT_NODE * (conducted_ref[...] + gained)
 
 
 def mid_sums_kernel(
     own_ref, first_ref, enthalpy_ref, links_ref, cell_ref, node_ref,
-    enthalpy_out_ref, heat_ref, surface_ref, warmth_ref,
-):
-    enthalpy = node_part(own_ref, first_ref, first_ref, 6, enthalpy_ref, links_ref, node_ref)
+    enthalpy_out_ref, heat_ref, surface_ref, warmth_ref, conducted_ref,
+):
+    enthalpy = node_part(
+        own_ref, first_ref, first_ref, 6, enthalpy_ref, links_ref, node_ref, warmth_ref,
+        conducted_ref,
+    )
     enthalpy_out_ref[...] = enthalpy
     warmth_ref[...] = node_temp(enthalpy)
     heat_part(
@@ -337,23 +350,27 @@
         next_ref[pl.ds(2 + half, PAIRS, stride=4), :] = surface_ref[pl.ds(half, PAIRS, stride=2), :]
 
     def body(g, carry):
-        start = pl.multiple_of(g * 32, 32)
-        pack_air(air_out_ref, turned_ref, cell_ref, own_ref, next_ref, 4, start, 32, 3)
-        send_out(next_ref, (packed_out,), out_sems, 4, start, 32)
+        start = pl.multiple_of(g * 64, 64)
+        pack_air(air_out_ref, turned_ref, cell_ref, own_ref, next_ref, 4, start, 64, 6)
+        send_out(next_ref, (packed_out,), out_sems, 4, start, 64)
         return carry
 
-    lax.fori_loop(0, PAIRS // 32, body, 0)
+    lax.fori_loop(0, PAIRS // 64, body, 0)
     wait_out(next_ref, (packed_out,), out_sems)
 
 
 def post_sums_kernel(
     kept_ref, own_ref, received_ref, first_ref, enthalpy_ref, links_ref, cell_ref, node_ref,
-    enthalpy_out_ref, heat_ref,
-):
-    enthalpy_out_ref[...] = node_part(
-        own_ref, received_ref, first_ref, 4, enthalpy_ref, links_ref, node_ref
-    )
+    enthalpy_out, heat_ref, warmth_ref, conducted_ref, last_ref, sem,
+):
+    last_ref[...] = node_part(
+        own_ref, received_ref, first_ref, 4, enthalpy_ref, links_ref, node_ref, warmth_ref,
+        conducted_ref,
+    )
+    copy = pltpu.make_async_copy(last_ref, enthalpy_out, sem)
+    copy.start()
     heat_part(own_ref, received_ref, kept_ref, 4, cell_ref, heat_ref)
+    copy.wait()
 
 
 def post_air_kernel(
@@ -423,7 +440,7 @@
         "first_sums",
         [panel, block, (2 * PAIRS, LANES)],
         32,
-        scratch_shapes=[pltpu.VMEM(panel, F32)],
+        scratch_shapes=[pltpu.VMEM(panel, F32)] * 2,
     )(kept, first, enthalpy, adjacency_lists, cells, nodes)
     air, own, packed = call(
         mid_air_kernel,
@@ -438,7 +455,14 @@
     )(kept, heat, surface, air_temp, velocity, fluid, cells, *edges)
     received = exchange(packed)
     edges = halos(air)
-    enthalpy, heat = call(post_sums_kernel, "second_sums", [panel, block], 32)(
+    enthalpy, heat = call(
+        post_sums_kernel,
+        "second_sums",
+        [panel, block],
+        32,
+        out_specs=[HBM, VMEM],
+        scratch_shapes=[pltpu.VMEM(panel, F32)] * 3 + [pltpu.SemaphoreType.DMA],
+    )(
         kept, own, received, first, enthalpy, adjacency_lists, cells, nodes
     )
     (air,) = call(post_air_kernel, "second_air", [block], 32)(heat, air, velocity, fluid, *edges)

time: 64.5 us -> 63 us (0.977)
  Pallas kernels: 24.2 us -> 22.6 us
    pallas_call x1, Pallas kernels: 7.73 us -> 7.06 us  [local(): call(post_sums_kernel, 'second_sums', [panel, block], 32, out_specs=[HBM,...]
    pallas_call x1, Pallas kernels: 7.31 us -> 6.65 us  [local(): call(mid_sums_kernel, 'first_sums', [panel, block, (2 * PAIRS, LANES)], 3...]
  transfers between devices with their start and end apart: 10 -> 10, of which waited for: 2 -> 2; matrix products, arithmetic and copies ran while one was open for 0% -> 0% of each run, Pallas kernels for 23% -> 22%
where the time goes in v5:
time: 63 us; the launch traced here: 62.8 us
  starting transfers between devices  30.8 us (49%)
  Pallas kernels  22.6 us (36%)
  waiting for transfers between devices  8.35 us (13%)
  between operations  0.86 us (1%)
    all_to_all x2, starting transfers between devices, exchange(): lax.all_to_all(both, ('len', 'hgt'), split_axis=0, concat_axis=0, tiled=T...  16.2 us
    ppermute x4, starting transfers between devices, halos(): out.append(lax.ppermute(head, axis, [(j, i) for i, j in ring]))  12.3 us
    all_to_all x2, waiting for transfers between devices, exchange(): lax.all_to_all(both, ('len', 'hgt'), split_axis=0, concat_axis=0, tiled=T...  8.33 us
    pallas_call x1, Pallas kernels, local(): call(post_sums_kernel, 'second_sums', [panel, block], 32, out_specs=[HBM,...  7.06 us
    pallas_call x1, Pallas kernels, local(): call(mid_sums_kernel, 'first_sums', [panel, block, (2 * PAIRS, LANES)], 3...  6.65 us
    pallas_call x1, Pallas kernels, local(): call(pre_kernel, 'pack_first', [wide, wide], 60, in_specs=[HBM] * len(arr...  5.04 us
    pallas_call x1, Pallas kernels, local(): call(mid_air_kernel, 'first_air', [block, narrow, narrow], 32, out_specs=...  3.14 us
    ppermute x4, starting transfers between devices, halos(): out.append(lax.ppermute(tail, axis, ring))  2.32 us
  transfers between devices with their start and end apart: 10, of which 2 were waited for; matrix products, arithmetic and copies ran while one was open for 0% of the time, Pallas kernels for 22%

profile of v5, /device:TPU:1, one launch (start us, length us, event | category | flops | bytes accessed | tf_op | source)
XLA Modules:
  0.0 62.8 jit_solution(3597518685860960781)
XLA Ops:
  0.6 0.0 copy-start.4
  0.6 5.0 %pack_first.1 = (f32[768,128]{1,0:T(8,128)}, f32[768,128]{1,0:T(8,128)}) custom-call(f32[8,8,256]{2,1,0:T(8,128)} %air_ref.1, f32[32,128]{1,0:T(8,128)} %enthalpy_ref.1, s32[128,256]{1,0:T(8,128)} %bitcast.9, f32[128,256]{1,0:T(8,128)} %bitcast.18, s32[1,128]{1,0:T(1,128)} %rows_in.1, s32[128,256]{1,0:T(8,128)} %bitcast.13), custom_call_target="tpu_custom_call" | custom-call | tf_op jit(solution)/shard_map/pack_first/pallas_call | solution.py:425
  5.7 0.0 copy-start
  5.7 0.0 copy-start.1
  5.7 0.0 copy-start.2
  5.7 0.0 copy-start.3
  5.7 11.5 %all-to-all-start = ((f32[128,1,768]{2,1,0:T(1,128)}), f32[128,1,768]{2,1,0:T(1,128)S(1)}, u32[]{:S(2)}, u32[]{:S(2)}) async-start(f32[128,1,768]{2,1,0:T(1,128)} %bitcast.17), calls=%async_computation | async-start | bytes 786432 | tf_op jit(solution)/shard_map/all_to_all | solution.py:414
  17.2 0.0 copy-done.4
  17.3 5.5 %collective-permute-start.3 = (f32[8,1,256]{2,1,0:T(1,128)S(1)}, f32[8,1,256]{2,1,0:T(1,128)S(1)}, u32[]{:S(2)}, u32[]{:S(2)}) collective-permute-start(f32[8,1,256]{2,1,0:T(1,128)S(1)} %get-tuple-element.26), channel_id=1, source_target_pairs={{1,0},{2,1},{3,2},{4,3},{5,4},{6,5},{7,6},{8,7},{9,8},{10,9},{11,1... | collective-permute-start | bytes 24584 | tf_op jit(solution)/shard_map/ppermute | solution.py:408
  22.8 0.0 copy-start.7
  22.8 0.0 collective-permute-start.2
  22.8 0.6 %collective-permute-start.1 = (f32[1,8,256]{2,1,0:T(8,128)S(1)}, f32[1,8,256]{2,1,0:T(8,128)S(1)}, u32[]{:S(2)}, u32[]{:S(2)}) collective-permute-start(f32[1,8,256]{2,1,0:T(8,128)S(1)} %get-tuple-element.28), channel_id=1, source_target_pairs={{16,0},{32,16},{48,32},{64,48},{80,64},{96,80},{112,96},{0,112},{1... | collective-permute-start | bytes 24584 | tf_op jit(solution)/shard_map/ppermute | solution.py:408
  23.4 1.2 %collective-permute-start = (f32[1,8,256]{2,1,0:T(8,128)S(1)}, f32[1,8,256]{2,1,0:T(8,128)S(1)}, u32[]{:S(2)}, u32[]{:S(2)}) collective-permute-start(f32[1,8,256]{2,1,0:T(8,128)S(1)} %get-tuple-element.29), channel_id=1, source_target_pairs={{0,16},{16,32},{32,48},{48,64},{64,80},{80,96},{96,112},{112,0},{1... | collective-permute-start | bytes 24584 | tf_op jit(solution)/shard_map/ppermute | solution.py:407
  24.6 4.8 %all-to-all-done = f32[128,1,768]{2,1,0:T(1,128)S(1)} async-done(((f32[128,1,768]{2,1,0:T(1,128)}), f32[128,1,768]{2,1,0:T(1,128)S(1)}, u32[]{:S(2)}, u32[]{:S(2)}) %all-to-all-start) | async-done | bytes 393248 | tf_op jit(solution)/shard_map/all_to_all | solution.py:414
  29.4 0.0 copy-done
  29.4 0.0 copy-done.1
  29.4 0.0 copy-done.2
  29.4 0.0 copy-done.3
  29.4 0.0 copy-done.7
  29.4 0.0 copy-start.5
  29.4 0.0 copy-start.6
  29.4 6.6 %first_sums.1 = (f32[32,128]{1,0:T(8,128)S(1)}, f32[8,8,256]{2,1,0:T(8,128)S(1)}, f32[256,128]{1,0:T(8,128)S(1)}) custom-call(f32[768,128]{1,0:T(8,128)S(1)} %copy-done, f32[768,128]{1,0:T(8,128)S(1)} %bitcast.7, f32[32,128]{1,0:T(8,128)S(1)} %copy-done.7, s32[32,8,128]{2,1,0:T(8,128)S(1)} %copy-done.3, s32[128,256]{1,0:T(8,128)S(1)} %bitcast.10, ...), custom_call_target="tpu_custom_call" | custom-call | tf_op jit(solution)/shard_map/first_sums/pallas_call | solution.py:438
  36.1 0.0 collective-permute-done.3.right_ref
  36.1 0.0 collective-permute-done.2.left_ref
  36.1 0.0 collective-permute-done.1.ahead_ref
  36.1 0.0 collective-permute-done.behind_ref
  36.1 0.0 copy-done.5
  36.1 0.0 copy-done.6
  36.1 3.1 %first_air.1 = (f32[8,8,256]{2,1,0:T(8,128)S(1)}, f32[512,128]{1,0:T(8,128)S(1)}, f32[512,128]{1,0:T(8,128)}) custom-call(f32[768,128]{1,0:T(8,128)S(1)} %copy-done, f32[8,8,256]{2,1,0:T(8,128)S(1)} %get-tuple-element.14.heat_ref, f32[256,128]{1,0:T(8,128)S(1)} %get-tuple-element.15.surface_ref, f32[8,8,256]{2,1,0:T(8,128)S(1)} %copy-done.4, ...), custom_call_target="tpu_custom_call" | custom-call | tf_op jit(solution)/shard_map/first_air/pallas_call | solution.py:445
  39.3 4.7 %all-to-all-start.1 = ((f32[128,1,512]{2,1,0:T(1,128)}), f32[128,1,512]{2,1,0:T(1,128)S(1)}, u32[]{:S(2)}, u32[]{:S(2)}) async-start(f32[128,1,512]{2,1,0:T(1,128)} %bitcast.5), calls=%async_computation.1 | async-start | bytes 524288 | tf_op jit(solution)/shard_map/all_to_all | solution.py:414
  44.0 5.5 %collective-permute-start.7 = (f32[8,1,256]{2,1,0:T(1,128)S(1)}, f32[8,1,256]{2,1,0:T(1,128)S(1)}, u32[]{:S(2)}, u32[]{:S(2)}) collective-permute-start(f32[8,1,256]{2,1,0:T(1,128)S(1)} %get-tuple-element.22), channel_id=1, source_target_pairs={{1,0},{2,1},{3,2},{4,3},{5,4},{6,5},{7,6},{8,7},{9,8},{10,9},{11,1... | collective-permute-start | bytes 24584 | tf_op jit(solution)/shard_map/ppermute | solution.py:408
  49.5 0.0 collective-permute-start.6
  49.5 0.6 %collective-permute-start.5 = (f32[1,8,256]{2,1,0:T(8,128)S(1)}, f32[1,8,256]{2,1,0:T(8,128)S(1)}, u32[]{:S(2)}, u32[]{:S(2)}) collective-permute-start(f32[1,8,256]{2,1,0:T(8,128)S(1)} %get-tuple-element.24), channel_id=1, source_target_pairs={{16,0},{32,16},{48,32},{64,48},{80,64},{96,80},{112,96},{0,112},{1... | collective-permute-start | bytes 24584 | tf_op jit(solution)/shard_map/ppermute | solution.py:408
  50.2 1.2 %collective-permute-start.4 = (f32[1,8,256]{2,1,0:T(8,128)S(1)}, f32[1,8,256]{2,1,0:T(8,128)S(1)}, u32[]{:S(2)}, u32[]{:S(2)}) collective-permute-start(f32[1,8,256]{2,1,0:T(8,128)S(1)} %get-tuple-element.25), channel_id=1, source_target_pairs={{0,16},{16,32},{32,48},{48,64},{64,80},{80,96},{96,112},{112,0},{1... | collective-permute-start | bytes 24584 | tf_op jit(solution)/shard_map/ppermute | solution.py:407
  51.3 3.5 %all-to-all-done.1 = f32[128,1,512]{2,1,0:T(1,128)S(1)} async-done(((f32[128,1,512]{2,1,0:T(1,128)}), f32[128,1,512]{2,1,0:T(1,128)S(1)}, u32[]{:S(2)}, u32[]{:S(2)}) %all-to-all-start.1) | async-done | bytes 262176 | tf_op jit(solution)/shard_map/all_to_all | solution.py:414
  54.9 7.1 %second_sums.1 = (f32[32,128]{1,0:T(8,128)}, f32[8,8,256]{2,1,0:T(8,128)S(1)}) custom-call(f32[768,128]{1,0:T(8,128)S(1)} %copy-done, f32[512,128]{1,0:T(8,128)S(1)} %get-tuple-element.16.own_ref, f32[512,128]{1,0:T(8,128)S(1)} %bitcast.16, f32[768,128]{1,0:T(8,128)S(1)} %bitcast.8, f32[32,128]{1,0:T(8,128)S(1)} %get-tuple-element.18.enthalpy_ref, ...), custom_call_target="tpu_custom_call" | custom-call | tf_op jit(solution)/shard_map/second_sums/pallas_call | solution.py:458
  62.0 0.0 collective-permute-done.7.right_ref
  62.0 0.0 collective-permute-done.6.left_ref
  62.0 0.0 collective-permute-done.5.ahead_ref
  62.0 0.0 collective-permute-done.4.behind_ref
  62.0 0.8 %second_air.1 = f32[8,8,256]{2,1,0:T(8,128)} custom-call(f32[8,8,256]{2,1,0:T(8,128)S(1)} %get-tuple-element.19.heat_ref, f32[8,8,256]{2,1,0:T(8,128)S(1)} %get-tuple-element.20.air_ref, f32[8,8,256]{2,1,0:T(8,128)S(1)} %copy-done.5, s32[8,8,256]{2,1,0:T(8,128)S(1)} %copy-done.6, f32[1,8,256]{2,1,0:T(8,128)S(1)} %collective-permute-done.4.behind_ref, ...), custom_call_target="tpu_custom_call" | custom-call | tf_op jit(solution)/shard_map/second_air/pallas_call | solution.py:468
  (4 shorter events, 0.0 us)
Async XLA Ops:
  0.6 16.6 %copy-start.4 = (f32[8,8,256]{2,1,0:T(8,128)S(1)}, f32[8,8,256]{2,1,0:T(8,128)}, u32[]{:S(2)}) copy-start(f32[8,8,256]{2,1,0:T(8,128)} %air_ref.1) | copy-start | bytes 196612
  5.7 23.7 %copy-start = (f32[768,128]{1,0:T(8,128)S(1)}, f32[768,128]{1,0:T(8,128)}, u32[]{:S(2)}) copy-start(f32[768,128]{1,0:T(8,128)} %get-tuple-element.12.own_ref.kept_ref) | copy-start | bytes 1179652
  5.7 23.7 %copy-start.1 = (s32[1,128,256]{2,1,0:T(8,128)S(1)}, s32[1,128,256]{2,1,0:T(8,128)}, u32[]{:S(2)}) copy-start(s32[1,128,256]{2,1,0:T(8,128)} %param.14) | copy-start | bytes 393220
  5.7 23.7 %copy-start.2 = (s32[1,128,256]{2,1,0:T(8,128)S(1)}, s32[1,128,256]{2,1,0:T(8,128)}, u32[]{:S(2)}) copy-start(s32[1,128,256]{2,1,0:T(8,128)} %param.17) | copy-start | bytes 393220
  5.7 23.7 %copy-start.3 = (s32[32,8,128]{2,1,0:T(8,128)S(1)}, s32[32,8,128]{2,1,0:T(8,128)}, u32[]{:S(2)}) copy-start(s32[32,8,128]{2,1,0:T(8,128)} %links_ref.3) | copy-start | bytes 393220
  5.7 23.6 %all-to-all-start = ((f32[128,1,768]{2,1,0:T(1,128)}), f32[128,1,768]{2,1,0:T(1,128)S(1)}, u32[]{:S(2)}, u32[]{:S(2)}) async-start(f32[128,1,768]{2,1,0:T(1,128)} %bitcast.17), calls=%async_computation | async-start | bytes 786432 | tf_op jit(solution)/shard_map/all_to_all | solution.py:414
  17.3 18.8 %collective-permute-start.3 = (f32[8,1,256]{2,1,0:T(1,128)S(1)}, f32[8,1,256]{2,1,0:T(1,128)S(1)}, u32[]{:S(2)}, u32[]{:S(2)}) collective-permute-start(f32[8,1,256]{2,1,0:T(1,128)S(1)} %get-tuple-element.26), channel_id=1, source_target_pairs={{1,0},{2,1},{3,2},{4,3},{5,4},{6,5},{7,6},{8,7},{9,8},{10,9},{11,1... | collective-permute-start | bytes 24584 | tf_op jit(solution)/shard_map/ppermute | solution.py:408
  22.8 6.6 %copy-start.7 = (f32[32,128]{1,0:T(8,128)S(1)}, f32[32,128]{1,0:T(8,128)}, u32[]{:S(2)}) copy-start(f32[32,128]{1,0:T(8,128)} %enthalpy_ref.1) | copy-start | bytes 49156
  22.8 13.3 %collective-permute-start.2 = (f32[8,1,256]{2,1,0:T(1,128)S(1)}, f32[8,1,256]{2,1,0:T(1,128)S(1)}, u32[]{:S(2)}, u32[]{:S(2)}) collective-permute-start(f32[8,1,256]{2,1,0:T(1,128)S(1)} %get-tuple-element.27), channel_id=1, source_target_pairs={{0,1},{1,2},{2,3},{3,4},{4,5},{5,6},{6,7},{7,8},{8,9},{9,10},{10,1... | collective-permute-start | bytes 24584 | tf_op jit(solution)/shard_map/ppermute | solution.py:407
  22.8 13.3 %collective-permute-start.1 = (f32[1,8,256]{2,1,0:T(8,128)S(1)}, f32[1,8,256]{2,1,0:T(8,128)S(1)}, u32[]{:S(2)}, u32[]{:S(2)}) collective-permute-start(f32[1,8,256]{2,1,0:T(8,128)S(1)} %get-tuple-element.28), channel_id=1, source_target_pairs={{16,0},{32,16},{48,32},{64,48},{80,64},{96,80},{112,96},{0,112},{1... | collective-permute-start | bytes 24584 | tf_op jit(solution)/shard_map/ppermute | solution.py:408
  23.4 12.7 %collective-permute-start = (f32[1,8,256]{2,1,0:T(8,128)S(1)}, f32[1,8,256]{2,1,0:T(8,128)S(1)}, u32[]{:S(2)}, u32[]{:S(2)}) collective-permute-start(f32[1,8,256]{2,1,0:T(8,128)S(1)} %get-tuple-element.29), channel_id=1, source_target_pairs={{0,16},{16,32},{32,48},{48,64},{64,80},{80,96},{96,112},{112,0},{1... | collective-permute-start | bytes 24584 | tf_op jit(solution)/shard_map/ppermute | solution.py:407
  29.4 6.7 %copy-start.5 = (f32[8,8,256]{2,1,0:T(8,128)S(1)}, f32[8,8,256]{2,1,0:T(8,128)}, u32[]{:S(2)}) copy-start(f32[8,8,256]{2,1,0:T(8,128)} %velocity_ref.3) | copy-start | bytes 196612
  29.4 6.7 %copy-start.6 = (s32[8,8,256]{2,1,0:T(8,128)S(1)}, s32[8,8,256]{2,1,0:T(8,128)}, u32[]{:S(2)}) copy-start(s32[8,8,256]{2,1,0:T(8,128)} %fluid_ref.3) | copy-start | bytes 196612
  39.3 15.6 %all-to-all-start.1 = ((f32[128,1,512]{2,1,0:T(1,128)}), f32[128,1,512]{2,1,0:T(1,128)S(1)}, u32[]{:S(2)}, u32[]{:S(2)}) async-start(f32[128,1,512]{2,1,0:T(1,128)} %bitcast.5), calls=%async_computation.1 | async-start | bytes 524288 | tf_op jit(solution)/shard_map/all_to_all | solution.py:414
  44.0 17.9 %collective-permute-start.7 = (f32[8,1,256]{2,1,0:T(1,128)S(1)}, f32[8,1,256]{2,1,0:T(1,128)S(1)}, u32[]{:S(2)}, u32[]{:S(2)}) collective-permute-start(f32[8,1,256]{2,1,0:T(1,128)S(1)} %get-tuple-element.22), channel_id=1, source_target_pairs={{1,0},{2,1},{3,2},{4,3},{5,4},{6,5},{7,6},{8,7},{9,8},{10,9},{11,1... | collective-permute-start | bytes 24584 | tf_op jit(solution)/shard_map/ppermute | solution.py:408
  49.5 12.4 %collective-permute-start.6 = (f32[8,1,256]{2,1,0:T(1,128)S(1)}, f32[8,1,256]{2,1,0:T(1,128)S(1)}, u32[]{:S(2)}, u32[]{:S(2)}) collective-permute-start(f32[8,1,256]{2,1,0:T(1,128)S(1)} %get-tuple-element.23), channel_id=1, source_target_pairs={{0,1},{1,2},{2,3},{3,4},{4,5},{5,6},{6,7},{7,8},{8,9},{9,10},{10,1... | collective-permute-start | bytes 24584 | tf_op jit(solution)/shard_map/ppermute | solution.py:407
  49.5 12.4 %collective-permute-start.5 = (f32[1,8,256]{2,1,0:T(8,128)S(1)}, f32[1,8,256]{2,1,0:T(8,128)S(1)}, u32[]{:S(2)}, u32[]{:S(2)}) collective-permute-start(f32[1,8,256]{2,1,0:T(8,128)S(1)} %get-tuple-element.24), channel_id=1, source_target_pairs={{16,0},{32,16},{48,32},{64,48},{80,64},{96,80},{112,96},{0,112},{1... | collective-permute-start | bytes 24584 | tf_op jit(solution)/shard_map/ppermute | solution.py:408
  50.2 11.8 %collective-permute-start.4 = (f32[1,8,256]{2,1,0:T(8,128)S(1)}, f32[1,8,256]{2,1,0:T(8,128)S(1)}, u32[]{:S(2)}, u32[]{:S(2)}) collective-permute-start(f32[1,8,256]{2,1,0:T(8,128)S(1)} %get-tuple-element.25), channel_id=1, source_target_pairs={{0,16},{16,32},{32,48},{48,64},{64,80},{80,96},{96,112},{112,0},{1... | collective-permute-start | bytes 24584 | tf_op jit(solution)/shard_map/ppermute | solution.py:407

commit v6 on v5

--- a/solution.py
+++ b/solution.py
@@ -359,28 +359,26 @@
     wait_out(next_ref, (packed_out,), out_sems)
 
 
-def post_sums_kernel(
+def post_kernel(
     kept_ref, own_ref, received_ref, first_ref, enthalpy_ref, links_ref, cell_ref, node_ref,
-    enthalpy_out, heat_ref, warmth_ref, conducted_ref, last_ref, sem,
-):
+    air_ref, velocity_ref, fluid_ref, behind_ref, ahead_ref, left_ref, right_ref,
+    air_out, enthalpy_out, heat_ref, warmth_ref, conducted_ref, last_ref, last_air_ref, sems,
+):
+    heat_part(own_ref, received_ref, kept_ref, 4, cell_ref, heat_ref)
+    air_part(
+        heat_ref, air_ref, velocity_ref, fluid_ref, (behind_ref, ahead_ref, left_ref, right_ref),
+        last_air_ref,
+    )
+    air_copy = pltpu.make_async_copy(last_air_ref, air_out, sems.at[0])
+    air_copy.start()
     last_ref[...] = node_part(
         own_ref, received_ref, first_ref, 4, enthalpy_ref, links_ref, node_ref, warmth_ref,
         conducted_ref,
     )
-    copy = pltpu.make_async_copy(last_ref, enthalpy_out, sem)
+    copy = pltpu.make_async_copy(last_ref, enthalpy_out, sems.at[1])
     copy.start()
-    heat_part(own_ref, received_ref, kept_ref, 4, cell_ref, heat_ref)
+    air_copy.wait()
     copy.wait()
-
-
-def post_air_kernel(
-    heat_ref, air_ref, velocity_ref, fluid_ref, behind_ref, ahead_ref, left_ref, right_ref,
-    air_out_ref,
-):
-    air_part(
-        heat_ref, air_ref, velocity_ref, fluid_ref, (behind_ref, ahead_ref, left_ref, right_ref),
-        air_out_ref,
-    )
 
 
 VMEM = pl.BlockSpec(memory_space=pltpu.VMEM)
@@ -455,17 +453,19 @@
     )(kept, heat, surface, air_temp, velocity, fluid, cells, *edges)
     received = exchange(packed)
     edges = halos(air)
-    enthalpy, heat = call(
-        post_sums_kernel,
-        "second_sums",
-        [panel, block],
+    air, enthalpy = call(
+        post_kernel,
+        "second_step",
+        [block, panel],
         32,
-        out_specs=[HBM, VMEM],
-        scratch_shapes=[pltpu.VMEM(panel, F32)] * 3 + [pltpu.SemaphoreType.DMA],
+        out_specs=[HBM, HBM],
+        scratch_shapes=[pltpu.VMEM(block, F32)]
+        + [pltpu.VMEM(panel, F32)] * 3
+        + [pltpu.VMEM(block, F32), pltpu.SemaphoreType.DMA((2,))],
     )(
-        kept, own, received, first, enthalpy, adjacency_lists, cells, nodes
-    )
-    (air,) = call(post_air_kernel, "second_air", [block], 32)(heat, air, velocity, fluid, *edges)
+        kept, own, received, first, enthalpy, adjacency_lists, cells, nodes, air, velocity, fluid,
+        *edges,
+    )
     return air, enthalpy
 
 

time: 63 us -> 63.6 us (level)
  waiting for transfers between devices: 8.35 us -> 9.06 us
    ppermute x4, waiting for transfers between devices: 0.01 us -> 4.25 us  [halos(): out.append(lax.ppermute(tail, axis, ring))]
    all_to_all x2, waiting for transfers between devices: 8.33 us -> 4.79 us  [exchange(): lax.all_to_all(both, ('len', 'hgt'), split_axis=0, concat_axis=0, tiled=T...]
    pallas_call x2 -> x1, Pallas kernels: 7.81 us -> 7.43 us  [local(): call(post_kernel, 'second_step', [block, panel], 32, out_specs=[HBM, HBM]...]
  transfers between devices with their start and end apart: 10 -> 10, of which waited for: 2 -> 2; matrix products, arithmetic and copies ran while one was open for 0% -> 0% of each run, Pallas kernels for 22% -> 11%
where the time goes in v6:
time: 63.6 us; the launch traced here: 63.2 us
  starting transfers between devices  30.8 us (48%)
  Pallas kernels  22.3 us (35%)
  waiting for transfers between devices  9.06 us (14%)
  between operations  0.99 us (2%)
    all_to_all x2, starting transfers between devices, exchange(): lax.all_to_all(both, ('len', 'hgt'), split_axis=0, concat_axis=0, tiled=T...  16.2 us
    ppermute x4, starting transfers between devices, halos(): out.append(lax.ppermute(head, axis, [(j, i) for i, j in ring]))  12.3 us
    pallas_call x1, Pallas kernels, local(): call(post_kernel, 'second_step', [block, panel], 32, out_specs=[HBM, HBM]...  7.43 us
    pallas_call x1, Pallas kernels, local(): call(mid_sums_kernel, 'first_sums', [panel, block, (2 * PAIRS, LANES)], 3...  6.66 us
    pallas_call x1, Pallas kernels, local(): call(pre_kernel, 'pack_first', [wide, wide], 60, in_specs=[HBM] * len(arr...  5.04 us
    all_to_all x2, waiting for transfers between devices, exchange(): lax.all_to_all(both, ('len', 'hgt'), split_axis=0, concat_axis=0, tiled=T...  4.79 us
    ppermute x4, waiting for transfers between devices, halos(): out.append(lax.ppermute(tail, axis, ring))  4.25 us
    pallas_call x1, Pallas kernels, local(): call(mid_air_kernel, 'first_air', [block, narrow, narrow], 32, out_specs=...  3.14 us
  transfers between devices with their start and end apart: 10, of which 2 were waited for; matrix products, arithmetic and copies ran while one was open for 0% of the time, Pallas kernels for 11%

profile of v6, /device:TPU:1, one launch (start us, length us, event | category | flops | bytes accessed | tf_op | source)
XLA Modules:
  0.0 63.2 jit_solution(12081031409378816889)
XLA Ops:
  0.6 0.0 copy-start.4
  0.6 5.0 %pack_first.1 = (f32[768,128]{1,0:T(8,128)}, f32[768,128]{1,0:T(8,128)}) custom-call(f32[8,8,256]{2,1,0:T(8,128)} %air_ref.1, f32[32,128]{1,0:T(8,128)} %enthalpy_ref.1, s32[128,256]{1,0:T(8,128)} %bitcast.9, f32[128,256]{1,0:T(8,128)} %bitcast.18, s32[1,128]{1,0:T(1,128)} %rows_in.1, s32[128,256]{1,0:T(8,128)} %bitcast.13), custom_call_target="tpu_custom_call" | custom-call | tf_op jit(solution)/shard_map/pack_first/pallas_call | solution.py:423
  5.7 0.0 copy-start
  5.7 0.0 copy-start.1
  5.7 0.0 copy-start.2
  5.7 0.0 copy-start.3
  5.7 11.5 %all-to-all-start = ((f32[128,1,768]{2,1,0:T(1,128)}), f32[128,1,768]{2,1,0:T(1,128)S(1)}, u32[]{:S(2)}, u32[]{:S(2)}) async-start(f32[128,1,768]{2,1,0:T(1,128)} %bitcast.17), calls=%async_computation | async-start | bytes 786432 | tf_op jit(solution)/shard_map/all_to_all | solution.py:412
  17.2 0.0 copy-done.4
  17.3 5.5 %collective-permute-start.3 = (f32[8,1,256]{2,1,0:T(1,128)S(1)}, f32[8,1,256]{2,1,0:T(1,128)S(1)}, u32[]{:S(2)}, u32[]{:S(2)}) collective-permute-start(f32[8,1,256]{2,1,0:T(1,128)S(1)} %get-tuple-element.22), channel_id=1, source_target_pairs={{1,0},{2,1},{3,2},{4,3},{5,4},{6,5},{7,6},{8,7},{9,8},{10,9},{11,1... | collective-permute-start | bytes 24584 | tf_op jit(solution)/shard_map/ppermute | solution.py:406
  22.8 0.0 copy-start.7
  22.8 0.0 collective-permute-start.2
  22.8 0.6 %collective-permute-start.1 = (f32[1,8,256]{2,1,0:T(8,128)S(1)}, f32[1,8,256]{2,1,0:T(8,128)S(1)}, u32[]{:S(2)}, u32[]{:S(2)}) collective-permute-start(f32[1,8,256]{2,1,0:T(8,128)S(1)} %get-tuple-element.24), channel_id=1, source_target_pairs={{16,0},{32,16},{48,32},{64,48},{80,64},{96,80},{112,96},{0,112},{1... | collective-permute-start | bytes 24584 | tf_op jit(solution)/shard_map/ppermute | solution.py:406
  23.4 1.2 %collective-permute-start = (f32[1,8,256]{2,1,0:T(8,128)S(1)}, f32[1,8,256]{2,1,0:T(8,128)S(1)}, u32[]{:S(2)}, u32[]{:S(2)}) collective-permute-start(f32[1,8,256]{2,1,0:T(8,128)S(1)} %get-tuple-element.25), channel_id=1, source_target_pairs={{0,16},{16,32},{32,48},{48,64},{64,80},{80,96},{96,112},{112,0},{1... | collective-permute-start | bytes 24584 | tf_op jit(solution)/shard_map/ppermute | solution.py:405
  24.6 4.8 %all-to-all-done = f32[128,1,768]{2,1,0:T(1,128)S(1)} async-done(((f32[128,1,768]{2,1,0:T(1,128)}), f32[128,1,768]{2,1,0:T(1,128)S(1)}, u32[]{:S(2)}, u32[]{:S(2)}) %all-to-all-start) | async-done | bytes 393248 | tf_op jit(solution)/shard_map/all_to_all | solution.py:412
  29.4 0.0 copy-done
  29.4 0.0 copy-done.1
  29.4 0.0 copy-done.2
  29.4 0.0 copy-done.3
  29.4 0.0 copy-done.7
  29.4 0.0 copy-start.5
  29.4 0.0 copy-start.6
  29.4 6.7 %first_sums.1 = (f32[32,128]{1,0:T(8,128)S(1)}, f32[8,8,256]{2,1,0:T(8,128)S(1)}, f32[256,128]{1,0:T(8,128)S(1)}) custom-call(f32[768,128]{1,0:T(8,128)S(1)} %copy-done, f32[768,128]{1,0:T(8,128)S(1)} %bitcast.7, f32[32,128]{1,0:T(8,128)S(1)} %copy-done.7, s32[32,8,128]{2,1,0:T(8,128)S(1)} %copy-done.3, s32[128,256]{1,0:T(8,128)S(1)} %bitcast.10, ...), custom_call_target="tpu_custom_call" | custom-call | tf_op jit(solution)/shard_map/first_sums/pallas_call | solution.py:436
  36.1 0.0 collective-permute-done.3.right_ref
  36.1 0.0 collective-permute-done.2.left_ref
  36.1 0.0 collective-permute-done.1.ahead_ref
  36.1 0.0 collective-permute-done.behind_ref
  36.1 0.0 copy-done.5
  36.1 0.0 copy-done.6
  36.2 3.1 %first_air.1 = (f32[8,8,256]{2,1,0:T(8,128)S(1)}, f32[512,128]{1,0:T(8,128)S(1)}, f32[512,128]{1,0:T(8,128)}) custom-call(f32[768,128]{1,0:T(8,128)S(1)} %copy-done, f32[8,8,256]{2,1,0:T(8,128)S(1)} %get-tuple-element.12.heat_ref, f32[256,128]{1,0:T(8,128)S(1)} %get-tuple-element.13.surface_ref, f32[8,8,256]{2,1,0:T(8,128)S(1)} %copy-done.4, ...), custom_call_target="tpu_custom_call" | custom-call | tf_op jit(solution)/shard_map/first_air/pallas_call | solution.py:443
  39.3 4.7 %all-to-all-start.1 = ((f32[128,1,512]{2,1,0:T(1,128)}), f32[128,1,512]{2,1,0:T(1,128)S(1)}, u32[]{:S(2)}, u32[]{:S(2)}) async-start(f32[128,1,512]{2,1,0:T(1,128)} %bitcast.5), calls=%async_computation.1 | async-start | bytes 524288 | tf_op jit(solution)/shard_map/all_to_all | solution.py:412
  44.1 5.5 %collective-permute-start.7 = (f32[8,1,256]{2,1,0:T(1,128)S(1)}, f32[8,1,256]{2,1,0:T(1,128)S(1)}, u32[]{:S(2)}, u32[]{:S(2)}) collective-permute-start(f32[8,1,256]{2,1,0:T(1,128)S(1)} %get-tuple-element.18), channel_id=1, source_target_pairs={{1,0},{2,1},{3,2},{4,3},{5,4},{6,5},{7,6},{8,7},{9,8},{10,9},{11,1... | collective-permute-start | bytes 24584 | tf_op jit(solution)/shard_map/ppermute | solution.py:406
  49.5 0.0 collective-permute-start.6
  49.6 0.6 %collective-permute-start.5 = (f32[1,8,256]{2,1,0:T(8,128)S(1)}, f32[1,8,256]{2,1,0:T(8,128)S(1)}, u32[]{:S(2)}, u32[]{:S(2)}) collective-permute-start(f32[1,8,256]{2,1,0:T(8,128)S(1)} %get-tuple-element.20), channel_id=1, source_target_pairs={{16,0},{32,16},{48,32},{64,48},{80,64},{96,80},{112,96},{0,112},{1... | collective-permute-start | bytes 24584 | tf_op jit(solution)/shard_map/ppermute | solution.py:406
  50.2 1.2 %collective-permute-start.4 = (f32[1,8,256]{2,1,0:T(8,128)S(1)}, f32[1,8,256]{2,1,0:T(8,128)S(1)}, u32[]{:S(2)}, u32[]{:S(2)}) collective-permute-start(f32[1,8,256]{2,1,0:T(8,128)S(1)} %get-tuple-element.21), channel_id=1, source_target_pairs={{0,16},{16,32},{32,48},{48,64},{64,80},{80,96},{96,112},{112,0},{1... | collective-permute-start | bytes 24584 | tf_op jit(solution)/shard_map/ppermute | solution.py:405
  51.4 0.0 collective-permute-done.7.right_ref
  51.4 4.2 %collective-permute-done.6.left_ref = f32[8,1,256]{2,1,0:T(1,128)S(1)} collective-permute-done((f32[8,1,256]{2,1,0:T(1,128)S(1)}, f32[8,1,256]{2,1,0:T(1,128)S(1)}, u32[]{:S(2)}, u32[]{:S(2)}) %collective-permute-start.6) | collective-permute-done | bytes 8224 | tf_op jit(solution)/shard_map/ppermute | solution.py:405
  55.6 0.0 collective-permute-done.5.ahead_ref
  55.6 0.0 collective-permute-done.4.behind_ref
  55.6 0.0 all-to-all-done.1
  55.6 7.4 %second_step.1 = (f32[8,8,256]{2,1,0:T(8,128)}, f32[32,128]{1,0:T(8,128)}) custom-call(f32[768,128]{1,0:T(8,128)S(1)} %copy-done, f32[512,128]{1,0:T(8,128)S(1)} %get-tuple-element.14.own_ref, f32[512,128]{1,0:T(8,128)S(1)} %bitcast.16, f32[768,128]{1,0:T(8,128)S(1)} %bitcast.8, f32[32,128]{1,0:T(8,128)S(1)} %get-tuple-element.16.enthalpy_ref, ...), custom_call_target="tpu_custom_call" | custom-call | tf_op jit(solution)/shard_map/second_step/pallas_call | solution.py:456
  (4 shorter events, 0.0 us)
Async XLA Ops:
  0.6 16.6 %copy-start.4 = (f32[8,8,256]{2,1,0:T(8,128)S(1)}, f32[8,8,256]{2,1,0:T(8,128)}, u32[]{:S(2)}) copy-start(f32[8,8,256]{2,1,0:T(8,128)} %air_ref.1) | copy-start | bytes 196612
  5.7 23.7 %copy-start = (f32[768,128]{1,0:T(8,128)S(1)}, f32[768,128]{1,0:T(8,128)}, u32[]{:S(2)}) copy-start(f32[768,128]{1,0:T(8,128)} %get-tuple-element.10.own_ref.kept_ref) | copy-start | bytes 1179652
  5.7 23.7 %copy-start.1 = (s32[1,128,256]{2,1,0:T(8,128)S(1)}, s32[1,128,256]{2,1,0:T(8,128)}, u32[]{:S(2)}) copy-start(s32[1,128,256]{2,1,0:T(8,128)} %param.14) | copy-start | bytes 393220
  5.7 23.7 %copy-start.2 = (s32[1,128,256]{2,1,0:T(8,128)S(1)}, s32[1,128,256]{2,1,0:T(8,128)}, u32[]{:S(2)}) copy-start(s32[1,128,256]{2,1,0:T(8,128)} %param.17) | copy-start | bytes 393220
  5.7 23.7 %copy-start.3 = (s32[32,8,128]{2,1,0:T(8,128)S(1)}, s32[32,8,128]{2,1,0:T(8,128)}, u32[]{:S(2)}) copy-start(s32[32,8,128]{2,1,0:T(8,128)} %links_ref.3) | copy-start | bytes 393220
  5.7 23.6 %all-to-all-start = ((f32[128,1,768]{2,1,0:T(1,128)}), f32[128,1,768]{2,1,0:T(1,128)S(1)}, u32[]{:S(2)}, u32[]{:S(2)}) async-start(f32[128,1,768]{2,1,0:T(1,128)} %bitcast.17), calls=%async_computation | async-start | bytes 786432 | tf_op jit(solution)/shard_map/all_to_all | solution.py:412
  17.3 18.8 %collective-permute-start.3 = (f32[8,1,256]{2,1,0:T(1,128)S(1)}, f32[8,1,256]{2,1,0:T(1,128)S(1)}, u32[]{:S(2)}, u32[]{:S(2)}) collective-permute-start(f32[8,1,256]{2,1,0:T(1,128)S(1)} %get-tuple-element.22), channel_id=1, source_target_pairs={{1,0},{2,1},{3,2},{4,3},{5,4},{6,5},{7,6},{8,7},{9,8},{10,9},{11,1... | collective-permute-start | bytes 24584 | tf_op jit(solution)/shard_map/ppermute | solution.py:406
  22.8 6.6 %copy-start.7 = (f32[32,128]{1,0:T(8,128)S(1)}, f32[32,128]{1,0:T(8,128)}, u32[]{:S(2)}) copy-start(f32[32,128]{1,0:T(8,128)} %enthalpy_ref.1) | copy-start | bytes 49156
  22.8 13.3 %collective-permute-start.2 = (f32[8,1,256]{2,1,0:T(1,128)S(1)}, f32[8,1,256]{2,1,0:T(1,128)S(1)}, u32[]{:S(2)}, u32[]{:S(2)}) collective-permute-start(f32[8,1,256]{2,1,0:T(1,128)S(1)} %get-tuple-element.23), channel_id=1, source_target_pairs={{0,1},{1,2},{2,3},{3,4},{4,5},{5,6},{6,7},{7,8},{8,9},{9,10},{10,1... | collective-permute-start | bytes 24584 | tf_op jit(solution)/shard_map/ppermute | solution.py:405
  22.8 13.3 %collective-permute-start.1 = (f32[1,8,256]{2,1,0:T(8,128)S(1)}, f32[1,8,256]{2,1,0:T(8,128)S(1)}, u32[]{:S(2)}, u32[]{:S(2)}) collective-permute-start(f32[1,8,256]{2,1,0:T(8,128)S(1)} %get-tuple-element.24), channel_id=1, source_target_pairs={{16,0},{32,16},{48,32},{64,48},{80,64},{96,80},{112,96},{0,112},{1... | collective-permute-start | bytes 24584 | tf_op jit(solution)/shard_map/ppermute | solution.py:406
  23.4 12.7 %collective-permute-start = (f32[1,8,256]{2,1,0:T(8,128)S(1)}, f32[1,8,256]{2,1,0:T(8,128)S(1)}, u32[]{:S(2)}, u32[]{:S(2)}) collective-permute-start(f32[1,8,256]{2,1,0:T(8,128)S(1)} %get-tuple-element.25), channel_id=1, source_target_pairs={{0,16},{16,32},{32,48},{48,64},{64,80},{80,96},{96,112},{112,0},{1... | collective-permute-start | bytes 24584 | tf_op jit(solution)/shard_map/ppermute | solution.py:405
  29.4 6.7 %copy-start.5 = (f32[8,8,256]{2,1,0:T(8,128)S(1)}, f32[8,8,256]{2,1,0:T(8,128)}, u32[]{:S(2)}) copy-start(f32[8,8,256]{2,1,0:T(8,128)} %velocity_ref.3) | copy-start | bytes 196612
  29.4 6.7 %copy-start.6 = (s32[8,8,256]{2,1,0:T(8,128)S(1)}, s32[8,8,256]{2,1,0:T(8,128)}, u32[]{:S(2)}) copy-start(s32[8,8,256]{2,1,0:T(8,128)} %fluid_ref.3) | copy-start | bytes 196612
  39.3 16.3 %all-to-all-start.1 = ((f32[128,1,512]{2,1,0:T(1,128)}), f32[128,1,512]{2,1,0:T(1,128)S(1)}, u32[]{:S(2)}, u32[]{:S(2)}) async-start(f32[128,1,512]{2,1,0:T(1,128)} %bitcast.5), calls=%async_computation.1 | async-start | bytes 524288 | tf_op jit(solution)/shard_map/all_to_all | solution.py:412
  44.1 7.3 %collective-permute-start.7 = (f32[8,1,256]{2,1,0:T(1,128)S(1)}, f32[8,1,256]{2,1,0:T(1,128)S(1)}, u32[]{:S(2)}, u32[]{:S(2)}) collective-permute-start(f32[8,1,256]{2,1,0:T(1,128)S(1)} %get-tuple-element.18), channel_id=1, source_target_pairs={{1,0},{2,1},{3,2},{4,3},{5,4},{6,5},{7,6},{8,7},{9,8},{10,9},{11,1... | collective-permute-start | bytes 24584 | tf_op jit(solution)/shard_map/ppermute | solution.py:406
  49.5 6.1 %collective-permute-start.6 = (f32[8,1,256]{2,1,0:T(1,128)S(1)}, f32[8,1,256]{2,1,0:T(1,128)S(1)}, u32[]{:S(2)}, u32[]{:S(2)}) collective-permute-start(f32[8,1,256]{2,1,0:T(1,128)S(1)} %get-tuple-element.19), channel_id=1, source_target_pairs={{0,1},{1,2},{2,3},{3,4},{4,5},{5,6},{6,7},{7,8},{8,9},{9,10},{10,1... | collective-permute-start | bytes 24584 | tf_op jit(solution)/shard_map/ppermute | solution.py:405
  49.6 6.0 %collective-permute-start.5 = (f32[1,8,256]{2,1,0:T(8,128)S(1)}, f32[1,8,256]{2,1,0:T(8,128)S(1)}, u32[]{:S(2)}, u32[]{:S(2)}) collective-permute-start(f32[1,8,256]{2,1,0:T(8,128)S(1)} %get-tuple-element.20), channel_id=1, source_target_pairs={{16,0},{32,16},{48,32},{64,48},{80,64},{96,80},{112,96},{0,112},{1... | collective-permute-start | bytes 24584 | tf_op jit(solution)/shard_map/ppermute | solution.py:406
  50.2 5.4 %collective-permute-start.4 = (f32[1,8,256]{2,1,0:T(8,128)S(1)}, f32[1,8,256]{2,1,0:T(8,128)S(1)}, u32[]{:S(2)}, u32[]{:S(2)}) collective-permute-start(f32[1,8,256]{2,1,0:T(8,128)S(1)} %get-tuple-element.21), channel_id=1, source_target_pairs={{0,16},{16,32},{32,48},{48,64},{64,80},{80,96},{96,112},{112,0},{1... | collective-permute-start | bytes 24584 | tf_op jit(solution)/shard_map/ppermute | solution.py:405
